TPU v7x, 256 devices: a whole 4x4x8 slice. The times are simulated.
256 devices in a mesh: chan: 64 (over x, z, core), src: 4 (over y).
Axes of the slice: x: 4, y: 4, z: 8, core: 2. Of those that a mesh axis runs over, the one named last changes fastest.
Arguments:
- records: bfloat16 [8192, 4096], P('chan'), may hold values from -600 to 600
- virtual_sources: int32 [64], P('src'), may hold values from 0 to 8191
- pair_group: int32 [32768, 1], P(('chan', 'src')), may hold values from 0 to 63; in each aligned block of 128 rows (0 to 127, 128 to 255, ...) at most 4 rows name the same one
- pair_receiver: int32 [32768], P(('chan', 'src')), may hold values from 0 to 127
- pair_source: int32 [32768], P(('chan', 'src')), may hold values from 0 to 15
- observed: float32 [32768, 2048], P(('chan', 'src')), may hold values from -6 to 6
Outputs:
- adjoint_source: float32 [8192, 4096], P(('chan', 'src'))
- pair_misfit: float32 [32768], P(('chan', 'src'))
Inputs may be any that keep to these rules, and one draw needn't show every extreme that they name: `pair_group`: among the 128 pairs listed by one device at most 4 name the same channel group, and in every draw some device lists exactly 4 pairs for some group.
All inputs are finite; a program needn't handle non-finite values.
Results may differ from a plain program's by a relative error of at most 0.0021.
Values sent between devices are 32-bit elements; how exact they have to be, the bound alone decides.
A program may use at most 64 MiB of HBM per device.

v0:
```python
import math

import jax
import jax.numpy as jnp
from jax import lax
from jax.sharding import PartitionSpec as P

K0 = 64


def fourier_basis(offset, length, time_len, bin_count):
    sample_times = offset + jnp.arange(length, dtype=jnp.int32)[:, None]
    band_bins = K0 + jnp.arange(bin_count, dtype=jnp.int32)[None, :]
    phase_index = band_bins * sample_times % (2 * time_len)
    angles = phase_index.astype(jnp.float32) * (math.pi / time_len)
    return jnp.concatenate([jnp.cos(angles), -jnp.sin(angles)], axis=1)


def forward(signal_rows, bin_count):
    time_len = signal_rows.shape[1]
    block_len = min(512, time_len)

    def add_block(block_index, running):
        offset = block_index * block_len
        segment = lax.dynamic_slice_in_dim(signal_rows, offset, block_len, 1)
        fourier_table = fourier_basis(offset, block_len, time_len, bin_count).astype(jnp.bfloat16)
        return running + jnp.dot(segment, fourier_table, preferred_element_type=jnp.float32)

    return lax.fori_loop(
        0,
        time_len // block_len,
        add_block,
        jnp.zeros((signal_rows.shape[0], 2 * bin_count), jnp.float32),
    )


def inverse(spectral, time_len):
    bin_count = spectral.shape[1] // 2
    block_len = min(512, time_len)

    def fill_block(block_index, output):
        offset = block_index * block_len
        fourier_table = fourier_basis(offset, block_len, time_len, bin_count)
        values = lax.dot_general(
            spectral,
            fourier_table,
            (((1,), (1,)), ((), ())),
            precision=lax.Precision.HIGHEST,
            preferred_element_type=jnp.float32,
        ) * (1.0 / math.sqrt(bin_count))
        return lax.dynamic_update_slice_in_dim(output, values, offset, 1)

    return lax.fori_loop(
        0, time_len // block_len, fill_block, jnp.zeros((spectral.shape[0], time_len), jnp.float32)
    )


def whiten(spectra):
    bin_count = spectra.shape[1] // 2
    band_power = jnp.sum(spectra * spectra, axis=1, keepdims=True) / bin_count
    return spectra / jnp.sqrt(band_power + 1e-06)


def band_taper(bin_count):
    band_bins = jnp.arange(bin_count, dtype=jnp.int32).astype(jnp.float32)
    return 0.5 - 0.5 * jnp.cos((band_bins + 0.5) * (2.0 * math.pi / bin_count))


def pair_terms(source_rows, receiver_rows, observed_rows):
    bin_count = observed_rows.shape[-1] // 2
    weights = band_taper(bin_count)
    source_real = source_rows[..., :bin_count]
    source_imag = source_rows[..., bin_count:]
    receiver_real = receiver_rows[..., :bin_count]
    receiver_imag = receiver_rows[..., bin_count:]
    corr_real = source_real * receiver_real + source_imag * receiver_imag
    corr_imag = source_real * receiver_imag - source_imag * receiver_real
    diff_real = corr_real - observed_rows[..., :bin_count]
    diff_imag = corr_imag - observed_rows[..., bin_count:]
    misfit = jnp.sum(weights * (diff_real * diff_real + diff_imag * diff_imag), axis=-1) / (
        2 * bin_count
    )
    resid_real = weights * diff_real
    resid_imag = weights * diff_imag
    term_real = resid_real * source_real - resid_imag * source_imag
    term_imag = resid_real * source_imag + resid_imag * source_real
    return (misfit, jnp.concatenate([term_real, term_imag], axis=-1))


def per_device(records, virtual_sources, pair_group, pair_receiver, pair_source, observed):
    row_count, time_len = records.shape
    pair_count = observed.shape[0]
    bin_count = observed.shape[1] // 2
    groups = lax.axis_size("chan")
    capacity = 2 * pair_count // groups
    slot_total = groups * capacity
    chan_index = lax.axis_index("chan")
    local_rows = virtual_sources - chan_index * row_count
    inside = (local_rows >= 0) & (local_rows < row_count)
    safe_rows = jnp.clip(local_rows, 0, row_count - 1)
    whitened = whiten(forward(records, bin_count))
    picked = jnp.where(inside[:, None], jnp.take(whitened, safe_rows, axis=0), 0.0)
    sources = lax.psum(picked, "chan")
    destination = pair_group[:, 0]
    group_hits = (destination[:, None] == jnp.arange(groups, dtype=jnp.int32)[None, :]).astype(
        jnp.int32
    )
    slot_ranks = jnp.sum((jnp.cumsum(group_hits, axis=0) - 1) * group_hits, axis=1)
    slot_index = destination * capacity + slot_ranks
    send_receiver = (
        jnp.full((slot_total,), -1, jnp.int32)
        .at[slot_index]
        .set(pair_receiver)
        .reshape(groups, capacity)
    )
    request = lax.all_to_all(send_receiver, "chan", split_axis=0, concat_axis=0, tiled=True)
    found_rows = jnp.take(whitened, jnp.clip(request, 0, row_count - 1), axis=0)
    found_rows = jnp.where((request >= 0)[..., None], found_rows, 0.0)
    fetched = lax.all_to_all(found_rows, "chan", split_axis=0, concat_axis=0, tiled=True)
    receiver_rows = fetched.reshape(slot_total, 2 * bin_count)[slot_index]
    source_rows = jnp.take(sources, pair_source, axis=0)
    pair_misfit, adjoint_term = pair_terms(source_rows, receiver_rows, observed)
    send_terms = (
        jnp.zeros((slot_total, 2 * bin_count), jnp.float32)
        .at[slot_index]
        .set(adjoint_term)
        .reshape(groups, capacity, 2 * bin_count)
    )
    arrived_terms, receivers = (
        lax.all_to_all(send_terms, "chan", split_axis=0, concat_axis=0, tiled=True),
        lax.all_to_all(send_receiver, "chan", split_axis=0, concat_axis=0, tiled=True),
    )
    flat_terms = arrived_terms.reshape(slot_total, 2 * bin_count)
    flat_receivers = receivers.reshape(slot_total)
    selector = (jnp.arange(row_count, dtype=jnp.int32)[:, None] == flat_receivers[None, :]).astype(
        jnp.float32
    )
    adjoint_spectra = jnp.dot(
        selector, flat_terms, precision=lax.Precision.HIGHEST, preferred_element_type=jnp.float32
    )
    adjoint_source = lax.psum_scatter(
        inverse(adjoint_spectra, time_len), "src", scatter_dimension=0, tiled=True
    )
    return (adjoint_source, pair_misfit)


def solution(mesh):
    return jax.shard_map(
        per_device,
        mesh=mesh,
        in_specs=(
            P("chan", None),
            P("src"),
            P(("chan", "src"), None),
            P(("chan", "src")),
            P(("chan", "src")),
            P(("chan", "src"), None),
        ),
        out_specs=(P(("chan", "src"), None), P(("chan", "src"))),
        check_vma=False,
    )
```

profile of v0, /device:TPU:1, one launch (start us, length us, event | category | flops | bytes accessed | tf_op | source)
XLA Modules:
  0.0 526.5 jit_solution(5404071709264893560)
XLA Ops:
  11.4 13.0 %all-to-all-start = ((s32[64,1,4]{2,1,0:T(1,128)}), s32[64,1,4]{2,1,0:T(1,128)S(1)}, u32[]{:S(2)}, u32[]{:S(2)}) async-start(s32[64,1,4]{2,1,0:T(1,128)} %bitcast.4), calls=%async_computation | async-start | bytes 65536 | tf_op jit(solution)/shard_map/all_to_all | solution.py:131
  24.4 85.0 %while.32 = (s32[]{:T(128)}, f32[128,2048]{1,0:T(8,128)S(1)}, bf16[128,4096]{1,0:T(8,128)(2,1)}, s32[]{:T(128)}, s32[]{:T(128)}, /*index=5*/s32[]{:T(128)}, s32[]{:T(128)}) while((s32[]{:T(128)}, f32[128,2048]{1,0:T(8,128)S(1)}, bf16[128,4096]{1,0:T(8,128)(2,1)}, s32[]{:T(128)}, s32[]{:T(128)}, /*index=5*/s32[]{:T(128)}, ...), condition=%wide.region_4.5_spmd.clone, body=%wide.region_3.4_spmd.clone.sunk | while | flops 282068480 | bytes 6434965 | solution.py:29
  24.5 9.0 %cosine_convert_fusion.2 = (bf16[512,1024]{1,0:T(8,128)(2,1)S(1)}, bf16[512,1024]{1,0:T(8,128)(2,1)S(1)}) fusion(s32[512]{0:T(512)S(1)} %iota_add_fusion.10, s32[1024]{0:T(1024)S(1)} %iota_add_fusion.11), kind=kLoop, calls=%fused_computation.39.clone.1 | loop fusion | flops 8912896 | bytes 2103296 | tf_op jit(solution)/shard_map/convert
  35.1 9.0 %cosine_convert_fusion.2 = (bf16[512,1024]{1,0:T(8,128)(2,1)S(1)}, bf16[512,1024]{1,0:T(8,128)(2,1)S(1)}) fusion(s32[512]{0:T(512)S(1)} %iota_add_fusion.10, s32[1024]{0:T(1024)S(1)} %iota_add_fusion.11), kind=kLoop, calls=%fused_computation.39.clone.1 | loop fusion | flops 8912896 | bytes 2103296 | tf_op jit(solution)/shard_map/convert
  45.7 9.0 %cosine_convert_fusion.2 = (bf16[512,1024]{1,0:T(8,128)(2,1)S(1)}, bf16[512,1024]{1,0:T(8,128)(2,1)S(1)}) fusion(s32[512]{0:T(512)S(1)} %iota_add_fusion.10, s32[1024]{0:T(1024)S(1)} %iota_add_fusion.11), kind=kLoop, calls=%fused_computation.39.clone.1 | loop fusion | flops 8912896 | bytes 2103296 | tf_op jit(solution)/shard_map/convert
  56.3 9.0 %cosine_convert_fusion.2 = (bf16[512,1024]{1,0:T(8,128)(2,1)S(1)}, bf16[512,1024]{1,0:T(8,128)(2,1)S(1)}) fusion(s32[512]{0:T(512)S(1)} %iota_add_fusion.10, s32[1024]{0:T(1024)S(1)} %iota_add_fusion.11), kind=kLoop, calls=%fused_computation.39.clone.1 | loop fusion | flops 8912896 | bytes 2103296 | tf_op jit(solution)/shard_map/convert
  67.0 9.0 %cosine_convert_fusion.2 = (bf16[512,1024]{1,0:T(8,128)(2,1)S(1)}, bf16[512,1024]{1,0:T(8,128)(2,1)S(1)}) fusion(s32[512]{0:T(512)S(1)} %iota_add_fusion.10, s32[1024]{0:T(1024)S(1)} %iota_add_fusion.11), kind=kLoop, calls=%fused_computation.39.clone.1 | loop fusion | flops 8912896 | bytes 2103296 | tf_op jit(solution)/shard_map/convert
  77.6 9.0 %cosine_convert_fusion.2 = (bf16[512,1024]{1,0:T(8,128)(2,1)S(1)}, bf16[512,1024]{1,0:T(8,128)(2,1)S(1)}) fusion(s32[512]{0:T(512)S(1)} %iota_add_fusion.10, s32[1024]{0:T(1024)S(1)} %iota_add_fusion.11), kind=kLoop, calls=%fused_computation.39.clone.1 | loop fusion | flops 8912896 | bytes 2103296 | tf_op jit(solution)/shard_map/convert
  88.2 9.0 %cosine_convert_fusion.2 = (bf16[512,1024]{1,0:T(8,128)(2,1)S(1)}, bf16[512,1024]{1,0:T(8,128)(2,1)S(1)}) fusion(s32[512]{0:T(512)S(1)} %iota_add_fusion.10, s32[1024]{0:T(1024)S(1)} %iota_add_fusion.11), kind=kLoop, calls=%fused_computation.39.clone.1 | loop fusion | flops 8912896 | bytes 2103296 | tf_op jit(solution)/shard_map/convert
  98.8 9.0 %cosine_convert_fusion.2 = (bf16[512,1024]{1,0:T(8,128)(2,1)S(1)}, bf16[512,1024]{1,0:T(8,128)(2,1)S(1)}) fusion(s32[512]{0:T(512)S(1)} %iota_add_fusion.10, s32[1024]{0:T(1024)S(1)} %iota_add_fusion.11), kind=kLoop, calls=%fused_computation.39.clone.1 | loop fusion | flops 8912896 | bytes 2103296 | tf_op jit(solution)/shard_map/convert
  114.6 3.6 select_select_fusion
  118.1 10.6 %all-to-all-start.1 = ((f32[64,4,2048]{2,1,0:T(4,128)}), f32[64,4,2048]{2,1,0:T(4,128)}, u32[]{:S(2)}, u32[]{:S(2)}) async-start(f32[64,4,2048]{2,1,0:T(4,128)} %select_select_fusion), calls=%async_computation.1 | async-start | bytes 4194304 | tf_op jit(solution)/shard_map/all_to_all | solution.py:119
  130.4 183.6 %all-reduce.2.cloned.1.call-done = f32[16,2048]{1,0:T(8,128)} async-done(((f32[16,2048]{1,0:T(8,128)}), f32[16,2048]{1,0:T(8,128)}) %all-reduce.2.cloned.1.call-update) | async-done | bytes 131088 | tf_op jit(solution)/shard_map/psum | solution.py:103
  326.0 6.6 %all-to-all-start.2 = ((f32[64,4,2048]{2,1,0:T(4,128)}), f32[64,4,2048]{2,1,0:T(4,128)S(1)}, u32[]{:S(2)}, u32[]{:S(2)}) async-start(f32[64,4,2048]{2,1,0:T(4,128)} %reshape.107), calls=%async_computation.2 | async-start | bytes 4194304 | tf_op jit(solution)/shard_map/all_to_all | solution.py:130
  332.7 51.1 %all-to-all-done.2 = f32[64,4,2048]{2,1,0:T(4,128)S(1)} async-done(((f32[64,4,2048]{2,1,0:T(4,128)}), f32[64,4,2048]{2,1,0:T(4,128)S(1)}, u32[]{:S(2)}, u32[]{:S(2)}) %all-to-all-start.2) | async-done | bytes 2097184 | tf_op jit(solution)/shard_map/all_to_all | solution.py:130
  389.6 101.1 %while.31 = (s32[]{:T(128)}, f32[128,4096]{1,0:T(8,128)}, f32[128,2048]{1,0:T(8,128)S(1)}, s32[]{:T(128)}, s32[]{:T(128)}, /*index=5*/s32[]{:T(128)}, s32[]{:T(128)}) while((s32[]{:T(128)}, f32[128,4096]{1,0:T(8,128)}, f32[128,2048]{1,0:T(8,128)S(1)}, s32[]{:T(128)}, s32[]{:T(128)}, /*index=5*/s32[]{:T(128)}, s32[]{:T(128)}) %tuple.90), condition=%wide.region_9.10_spmd, body=%wide.region_8.9_spmd.sunk | while | flops 1619592704 | bytes 10760323 | solution.py:53
  389.7 8.3 %fusion.46 = (f32[512,1024]{1,0:T(8,128)S(1)}, f32[512,1024]{1,0:T(8,128)S(1)}) fusion(s32[512]{0:T(512)S(1)} %iota_add_fusion.8, s32[1024]{0:T(1024)S(1)} %iota_add_fusion.9), kind=kLoop, calls=%fused_computation.21.clone.1 | loop fusion | flops 7864320 | bytes 4200448 | tf_op jit(solution)/shard_map/while/body/eval_jaxpr/cos | solution.py:16
  398.0 3.4 fusion.47
  402.3 8.3 %fusion.46 = (f32[512,1024]{1,0:T(8,128)S(1)}, f32[512,1024]{1,0:T(8,128)S(1)}) fusion(s32[512]{0:T(512)S(1)} %iota_add_fusion.8, s32[1024]{0:T(1024)S(1)} %iota_add_fusion.9), kind=kLoop, calls=%fused_computation.21.clone.1 | loop fusion | flops 7864320 | bytes 4200448 | tf_op jit(solution)/shard_map/while/body/eval_jaxpr/cos | solution.py:16
  410.6 3.4 fusion.47
  415.0 8.3 %fusion.46 = (f32[512,1024]{1,0:T(8,128)S(1)}, f32[512,1024]{1,0:T(8,128)S(1)}) fusion(s32[512]{0:T(512)S(1)} %iota_add_fusion.8, s32[1024]{0:T(1024)S(1)} %iota_add_fusion.9), kind=kLoop, calls=%fused_computation.21.clone.1 | loop fusion | flops 7864320 | bytes 4200448 | tf_op jit(solution)/shard_map/while/body/eval_jaxpr/cos | solution.py:16
  427.6 8.3 %fusion.46 = (f32[512,1024]{1,0:T(8,128)S(1)}, f32[512,1024]{1,0:T(8,128)S(1)}) fusion(s32[512]{0:T(512)S(1)} %iota_add_fusion.8, s32[1024]{0:T(1024)S(1)} %iota_add_fusion.9), kind=kLoop, calls=%fused_computation.21.clone.1 | loop fusion | flops 7864320 | bytes 4200448 | tf_op jit(solution)/shard_map/while/body/eval_jaxpr/cos | solution.py:16
  435.9 3.4 fusion.47
  440.3 8.3 %fusion.46 = (f32[512,1024]{1,0:T(8,128)S(1)}, f32[512,1024]{1,0:T(8,128)S(1)}) fusion(s32[512]{0:T(512)S(1)} %iota_add_fusion.8, s32[1024]{0:T(1024)S(1)} %iota_add_fusion.9), kind=kLoop, calls=%fused_computation.21.clone.1 | loop fusion | flops 7864320 | bytes 4200448 | tf_op jit(solution)/shard_map/while/body/eval_jaxpr/cos | solution.py:16
  448.6 3.4 fusion.47
  452.9 8.3 %fusion.46 = (f32[512,1024]{1,0:T(8,128)S(1)}, f32[512,1024]{1,0:T(8,128)S(1)}) fusion(s32[512]{0:T(512)S(1)} %iota_add_fusion.8, s32[1024]{0:T(1024)S(1)} %iota_add_fusion.9), kind=kLoop, calls=%fused_computation.21.clone.1 | loop fusion | flops 7864320 | bytes 4200448 | tf_op jit(solution)/shard_map/while/body/eval_jaxpr/cos | solution.py:16
  461.2 3.4 fusion.47
  465.5 8.3 %fusion.46 = (f32[512,1024]{1,0:T(8,128)S(1)}, f32[512,1024]{1,0:T(8,128)S(1)}) fusion(s32[512]{0:T(512)S(1)} %iota_add_fusion.8, s32[1024]{0:T(1024)S(1)} %iota_add_fusion.9), kind=kLoop, calls=%fused_computation.21.clone.1 | loop fusion | flops 7864320 | bytes 4200448 | tf_op jit(solution)/shard_map/while/body/eval_jaxpr/cos | solution.py:16
  473.8 3.4 fusion.47
  478.1 8.3 %fusion.46 = (f32[512,1024]{1,0:T(8,128)S(1)}, f32[512,1024]{1,0:T(8,128)S(1)}) fusion(s32[512]{0:T(512)S(1)} %iota_add_fusion.8, s32[1024]{0:T(1024)S(1)} %iota_add_fusion.9), kind=kLoop, calls=%fused_computation.21.clone.1 | loop fusion | flops 7864320 | bytes 4200448 | tf_op jit(solution)/shard_map/while/body/eval_jaxpr/cos | solution.py:16
  486.5 3.4 fusion.47
  491.3 28.4 %reduce-scatter.2.cloned.1.call-done = f32[32,4096]{1,0:T(8,128)} async-done(((f32[128,4096]{1,0:T(8,128)}), f32[32,4096]{1,0:T(8,128)}) %reduce-scatter.2.cloned.1.call-update) | async-done | bytes 524304 | tf_op jit(solution)/shard_map/reduce_scatter | solution.py:141
  (110 shorter events, 52.1 us)
Async XLA Ops:
  11.4 98.4 %all-to-all-start = ((s32[64,1,4]{2,1,0:T(1,128)}), s32[64,1,4]{2,1,0:T(1,128)S(1)}, u32[]{:S(2)}, u32[]{:S(2)}) async-start(s32[64,1,4]{2,1,0:T(1,128)} %bitcast.4), calls=%async_computation | async-start | bytes 65536 | tf_op jit(solution)/shard_map/all_to_all | solution.py:131
  118.1 10.7 %copy-start = (s32[16]{0:T(128)S(1)}, s32[16]{0:T(128)}, u32[]{:S(2)}) copy-start(s32[16]{0:T(128)} %param.11) | copy-start | bytes 196
  118.1 12.2 %copy-start.1 = (s32[128]{0:T(128)S(1)}, s32[128]{0:T(128)}, u32[]{:S(2)}) copy-start(s32[128]{0:T(128)} %param.14) | copy-start | bytes 1540
  118.1 198.3 %all-to-all-start.1 = ((f32[64,4,2048]{2,1,0:T(4,128)}), f32[64,4,2048]{2,1,0:T(4,128)}, u32[]{:S(2)}, u32[]{:S(2)}) async-start(f32[64,4,2048]{2,1,0:T(4,128)} %select_select_fusion), calls=%async_computation.1 | async-start | bytes 4194304 | tf_op jit(solution)/shard_map/all_to_all | solution.py:119
  128.8 185.2 %all-reduce.2.cloned.1.call-start = ((), (), s32[]{:S(2)}) async-start(), calls=%async_computation.4 | async-start | bytes 262144 | tf_op jit(solution)/shard_map/psum | solution.py:103
  326.0 57.9 %all-to-all-start.2 = ((f32[64,4,2048]{2,1,0:T(4,128)}), f32[64,4,2048]{2,1,0:T(4,128)S(1)}, u32[]{:S(2)}, u32[]{:S(2)}) async-start(f32[64,4,2048]{2,1,0:T(4,128)} %reshape.107), calls=%async_computation.2 | async-start | bytes 4194304 | tf_op jit(solution)/shard_map/all_to_all | solution.py:130
  332.6 187.1 %reduce-scatter.2.cloned.1.call-start = ((), (), s32[]{:S(2)}) async-start(), calls=%async_computation.5 | async-start | bytes 2621440 | tf_op jit(solution)/shard_map/reduce_scatter | solution.py:141
Sparse Core Ops, SparseCore 0:
  133.7 180.2 all-reduce.1
  490.9 28.7 reduce-scatter.1
where the time goes:
time: 527 us
  waiting for transfers between devices  263 us (50%)
  other arithmetic  151 us (29%)
  matrix products  42.2 us (8%)
  starting transfers between devices  30.3 us (6%)
  local copies, waits for them, and re-layouts  24.8 us (5%)
  between operations  14.3 us (3%)
    psum x1, waiting for transfers between devices, per_device(): sources = lax.psum(picked, 'chan')  184 us
    another operation x8, other arithmetic  72.2 us
    cos x8, other arithmetic, fourier_basis(): return jnp.concatenate([jnp.cos(angles), -jnp.sin(angles)], axis=1)  66.4 us
    all_to_all x1, waiting for transfers between devices, per_device(): lax.all_to_all(send_terms, 'chan', split_axis=0, concat_axis=0, tiled=True)  51.1 us
    reduce_scatter x1, waiting for transfers between devices, per_device(): lax.psum_scatter(inverse(adjoint_spectra, time_len), 'src', scatter_dimen...  28.4 us
    dot_general x8, matrix products, fill_block(): lax.dot_general(spectral, fourier_table, (((1,), (1,)), ((), ())), precis...  27.4 us
    all_to_all x1, starting transfers between devices, per_device(): lax.all_to_all(send_receiver, 'chan', split_axis=0, concat_axis=0, tiled=...  13 us
    dot_general x8, matrix products, add_block(): jnp.dot(segment, fourier_table, preferred_element_type=jnp.float32)  12.3 us
  transfers between devices with their start and end apart: 5, of which 3 were waited for; matrix products, arithmetic and copies ran while one was open for 17% of the time, Pallas kernels for 0%

commit v1 on v0

v1 whole, which is shorter than its diff:
```python
import functools
import math

import jax
import jax.numpy as jnp
from jax import lax
from jax.experimental import pallas as pl
from jax.experimental.pallas import tpu as pltpu
from jax.sharding import PartitionSpec as P

K0 = 64
CAP = 4
STEP = 64
MESH = pl.DeviceIdType.MESH
F32 = jnp.float32
BF16 = jnp.bfloat16


def iota(shape, axis):
    return lax.broadcasted_iota(jnp.int32, shape, axis)


def one_hot(mask):
    return jnp.where(mask, 1.0, 0.0).astype(BF16)


def dot(left, right):
    return jnp.dot(left, right, preferred_element_type=F32)


def dot_t(left, right):
    return lax.dot_general(left, right, (((1,), (1,)), ((), ())), preferred_element_type=F32)


def halves(value):
    high = value.astype(BF16)
    return high, (value - high.astype(F32)).astype(BF16)


def dot2(left, pair):
    return dot(left, pair[0]) + dot(left, pair[1])


def kernel(
    n,
    m,
    chunks,
    rec_ref,
    vs_ref,
    grow_ref,
    gcol_ref,
    prec_ref,
    psrc_ref,
    obs_ref,
    out_ref,
    mis_ref,
    obs_send,
    obs_recv,
    meta_send,
    meta_recv,
    src_send,
    src_mid,
    src_part,
    src_recv,
    adj_send,
    adj_recv,
    mis_send,
    mis_recv,
    table,
    cos_a,
    sin_a,
    cos_b,
    sin_b,
    spec,
    white_hi,
    white_lo,
    g1_ref,
    g2_ref,
    g1t_ref,
    g2t_ref,
    h_ref,
    mis_acc,
    send_sems,
    recv_sems,
    rs_send,
    rs_recv,
):
    chans, time_len = rec_ref.shape
    pairs, width = obs_ref.shape
    bins = width // 2
    part = bins // chunks
    rows_out = chans // m
    sources = vs_ref.shape[0]
    slots = n * CAP
    rows = 2 * slots
    me = lax.axis_index("chan")
    owner = lax.axis_index("src")
    META, SRC1, SRC2, MIS = chunks, chunks + 1, chunks + 2, chunks + 3

    barrier = pltpu.get_barrier_semaphore()

    def greet(i, carry):
        pl.semaphore_signal(
            barrier, inc=1, device_id={"chan": lax.rem(me + i, n)}, device_id_type=MESH
        )
        return carry

    lax.fori_loop(1, n, greet, 0)
    for i in range(1, m):
        pl.semaphore_signal(
            barrier, inc=1, device_id={"src": lax.rem(owner + i, m)}, device_id_type=MESH
        )

    def spread(send, recv, sem):
        def one(i, carry):
            other = lax.rem(me + i, n)
            pltpu.make_async_remote_copy(
                src_ref=send(other),
                dst_ref=recv.at[me],
                send_sem=send_sems.at[sem],
                recv_sem=recv_sems.at[sem],
                device_id={"chan": other},
                device_id_type=MESH,
            ).start()
            return carry

        pltpu.make_async_copy(send(me), recv.at[me], recv_sems.at[sem]).start()
        lax.fori_loop(1, n, one, 0)

    def arrived(recv, sem):
        pltpu.make_async_copy(recv, recv, recv_sems.at[sem]).wait()

    def left(recv, sem):
        some = recv.at[pl.ds(0, n - 1)]
        pltpu.make_async_copy(some, some, send_sems.at[sem]).wait()

    grow = grow_ref[...]
    before = (gcol_ref[...] == grow) & (iota((pairs, pairs), 0) < iota((pairs, pairs), 1))
    rank = jnp.sum(jnp.where(before, 1, 0), axis=0, keepdims=True)
    slot = grow * CAP + rank
    row_id = iota((rows, 2 * pairs), 0)
    row_slot = (row_id >> 3) * CAP + (row_id & 3)
    col_id = iota((rows, 2 * pairs), 1)
    imag_row = (row_id >> 2) & 1
    imag_col = jnp.where(col_id >= pairs, 1, 0)
    slot2 = jnp.concatenate([slot, slot], axis=1)
    place = one_hot((slot2 == row_slot) & (imag_row == imag_col))
    for q in range(chunks):
        lo, hi = q * part, (q + 1) * part
        block = jnp.concatenate(
            [obs_ref[:, lo:hi], obs_ref[:, bins + lo : bins + hi]], axis=0
        )
        obs_send[q] = dot2(place, halves(block)).reshape(n, 8, part)

    pick = slot == iota((slots, pairs), 0)
    slot_recv = jnp.sum(
        jnp.where(pick, prec_ref[...].astype(F32) + 1.0, 0.0), axis=1, keepdims=True
    )
    slot_src = jnp.sum(jnp.where(pick, psrc_ref[...].astype(F32), 0.0), axis=1, keepdims=True)
    lane = iota((slots, 128), 1)
    slot_rank = iota((slots, 128), 0) & 3
    coded = jnp.where(lane == slot_rank, slot_recv, 0.0) + jnp.where(
        lane == slot_rank + CAP, slot_src, 0.0
    )
    fold = one_hot(iota((n, slots), 0) == (iota((n, slots), 1) >> 2))
    meta_send[...] = dot(fold, coded.astype(BF16)).reshape(n, 1, 128)

    pl.semaphore_wait(barrier, n - 1 + m - 1)

    spread(lambda g: meta_send.at[g], meta_recv, META)
    for q in range(min(2, chunks)):
        spread(lambda g, q=q: obs_send.at[q, g], obs_recv.at[q], q)

    unit = math.pi / time_len
    steps = time_len // STEP
    bin_b = K0 + iota((STEP, bins), 1)
    phase_b = (bin_b * iota((STEP, bins), 0)) & (2 * time_len - 1)
    angle_b = phase_b.astype(F32) * unit
    cos_b[...] = jnp.cos(angle_b)
    sin_b[...] = jnp.sin(angle_b)
    phase_a = ((K0 + iota((steps, bins), 1)) * (iota((steps, bins), 0) * STEP)) & (2 * time_len - 1)
    angle_a = phase_a.astype(F32) * unit
    cos_a[...] = jnp.cos(angle_a).reshape(steps, 1, bins)
    sin_a[...] = jnp.sin(angle_a).reshape(steps, 1, bins)

    def fill(i, carry):
        ca, sa = cos_a[i], sin_a[i]
        cb, sb = cos_b[...], sin_b[...]
        at = pl.ds(pl.multiple_of(i * STEP, STEP), STEP)
        table[at, 0:bins] = (ca * cb - sa * sb).astype(BF16)
        table[at, bins : 2 * bins] = (-(sa * cb) - ca * sb).astype(BF16)
        return carry

    lax.fori_loop(0, steps, fill, 0)

    cols = min(256, width)

    def transform(i, power):
        at = pl.ds(pl.multiple_of(i * cols, cols), cols)
        values = dot(rec_ref[...], table[:, at])
        spec[:, at] = values
        return power + jnp.sum(values * values, axis=1, keepdims=True)

    power = lax.fori_loop(0, width // cols, transform, jnp.zeros((chans, 1), F32))
    norm = jnp.sqrt(power / bins + 1e-6)

    local = vs_ref[...] - me * chans
    chosen = one_hot(iota((sources, chans), 1) == local)
    for q in range(chunks):
        for h in range(2):
            at = slice(h * bins + q * part, h * bins + (q + 1) * part)
            high, low = halves(spec[:, at] / norm)
            for y in range(m):
                to = slice((2 * y + h) * rows_out, (2 * y + h + 1) * rows_out)
                white_hi[q, to, :] = high[y * rows_out : (y + 1) * rows_out, :]
                white_lo[q, to, :] = low[y * rows_out : (y + 1) * rows_out, :]
            picked = dot(chosen, high) + dot(chosen, low)
            for c in range(part // 128):
                block = (h * bins + q * part) // 128 + c
                for r in range(sources // 4):
                    src_send[r * (width // 128) + block] = picked[
                        4 * r : 4 * r + 4, 128 * c : 128 * (c + 1)
                    ]

    spread(lambda g: src_send.at[g], src_mid, SRC1)
    for q in range(2, min(3, chunks)):
        spread(lambda g, q=q: obs_send.at[q, g], obs_recv.at[q], q)
    arrived(src_mid, SRC1)
    src_part[...] = jnp.sum(src_mid[...], axis=0)
    spread(lambda g: src_part, src_recv, SRC2)
    for q in range(3, chunks):
        spread(lambda g, q=q: obs_send.at[q, g], obs_recv.at[q], q)

    arrived(meta_recv, META)
    unfold = one_hot((iota((rows, n), 0) >> 3) == iota((rows, n), 1))
    spread_meta = dot(unfold, meta_recv[...].reshape(n, 128).astype(BF16))
    lane = iota((rows, 128), 1)
    row_rank = iota((rows, 128), 0) & 3
    named = jnp.sum(jnp.where(lane == row_rank, spread_meta, 0.0), axis=1, keepdims=True)
    receiver = named.astype(jnp.int32) - 1
    source = jnp.sum(
        jnp.where(lane == row_rank + CAP, spread_meta, 0.0), axis=1, keepdims=True
    ).astype(jnp.int32)
    shift = rows_out.bit_length() - 1
    position = (receiver >> shift) * (2 * rows_out) + (receiver & (rows_out - 1))
    wide = (rows, 2 * chans)
    imag = (iota((rows, 1), 0) >> 2) & 1
    valid = receiver >= 0
    near = jnp.where(valid, position + imag * rows_out, -1)
    far = jnp.where(valid, position + (1 - imag) * rows_out, -1)
    sign = (1 - 2 * imag).astype(F32)
    g1 = jnp.where(iota(wide, 1) == near, 1.0, 0.0)
    g2 = jnp.where(iota(wide, 1) == far, sign, 0.0)
    g1_ref[...] = g1.astype(BF16)
    g2_ref[...] = g2.astype(BF16)
    g1t_ref[...] = g1.T.astype(BF16)
    g2t_ref[...] = g2.T.astype(BF16)
    h_ref[...] = one_hot((iota((rows, sources), 1) == source) & valid)

    arrived(src_recv, SRC2)

    def source_block(start):
        blocks = []
        for c in range(part // 128):
            block = start // 128 + c
            blocks.append(
                jnp.concatenate(
                    [src_recv[r * (width // 128) + block] for r in range(sources // 4)], axis=0
                )
            )
        return jnp.concatenate(blocks, axis=1)

    mis_acc[...] = jnp.zeros_like(mis_acc)

    def inverse(q):
        pltpu.make_async_copy(adj_recv.at[q], adj_recv.at[q], rs_recv.at[q]).wait()
        total = adj_recv[q, 0]
        for y in range(1, m):
            total = total + adj_recv[q, y]
        high, low = halves(total * (1.0 / math.sqrt(bins)))
        real = jnp.concatenate([high[:rows_out], low[:rows_out]], axis=0)
        imaginary = jnp.concatenate([high[rows_out:], low[rows_out:]], axis=0)
        span = min(512, time_len)

        def one(i, carry):
            at = pl.ds(pl.multiple_of(i * span, span), span)
            both = dot_t(real, table[at, q * part : (q + 1) * part]) + dot_t(
                imaginary, table[at, bins + q * part : bins + (q + 1) * part]
            )
            values = both[:rows_out] + both[rows_out:]
            if q == 0:
                out_ref[:, at] = values
            else:
                out_ref[:, at] += values
            return carry

        lax.fori_loop(0, time_len // span, one, 0)

    for q in range(chunks):
        arrived(obs_recv.at[q], q)
        band = (q * part + iota((1, part), 1)).astype(F32)
        taper = 0.5 - 0.5 * jnp.cos((band + 0.5) * (2.0 * math.pi / bins))
        s_re = dot2(h_ref[...], halves(source_block(q * part)))
        s_im = dot2(h_ref[...], halves(source_block(bins + q * part)))
        w_hi, w_lo = white_hi[q], white_lo[q]
        near_rows = dot2(g1_ref[...], (w_hi, w_lo))
        far_rows = dot2(g2_ref[...], (w_hi, w_lo))
        diff = s_re * near_rows + s_im * far_rows - obs_recv[q].reshape(rows, part)
        resid = taper * diff
        squares = resid * diff
        folded = squares[:, :128]
        for c in range(1, part // 128):
            folded = folded + squares[:, 128 * c : 128 * (c + 1)]
        mis_acc[...] += folded
        adj_send[q] = (
            dot2(g1t_ref[...], halves(resid * s_re)) + dot2(g2t_ref[...], halves(resid * s_im))
        ).reshape(m, 2 * rows_out, part)
        pltpu.make_async_copy(
            adj_send.at[q, owner], adj_recv.at[q, owner], rs_recv.at[q]
        ).start()
        for i in range(1, m):
            other = lax.rem(owner + i, m)
            pltpu.make_async_remote_copy(
                src_ref=adj_send.at[q, other],
                dst_ref=adj_recv.at[q, owner],
                send_sem=rs_send.at[q],
                recv_sem=rs_recv.at[q],
                device_id={"src": other},
                device_id_type=MESH,
            ).start()
        if q == chunks - 1:
            total = jnp.sum(mis_acc[...], axis=1, keepdims=True) * (0.5 / bins)
            spread_out = jnp.where(lane == row_rank, total, 0.0)
            fold8 = one_hot(iota((n, rows), 0) == (iota((n, rows), 1) >> 3))
            mis_send[...] = dot2(fold8, halves(spread_out)).reshape(n, 1, 128)
            spread(lambda g: mis_send.at[g], mis_recv, MIS)
        if q >= 1:
            inverse(q - 1)
    inverse(chunks - 1)

    arrived(mis_recv, MIS)
    unfold4 = one_hot((iota((slots, n), 0) >> 2) == iota((slots, n), 1))
    back = dot2(unfold4, halves(mis_recv[...].reshape(n, 128)))
    column = jnp.sum(
        jnp.where(iota((slots, 128), 1) == (iota((slots, 128), 0) & 3), back, 0.0),
        axis=1,
        keepdims=True,
    )
    mis_ref[...] = jnp.sum(jnp.where(pick, column, 0.0), axis=0, keepdims=True)

    for q in range(chunks):
        left(obs_recv.at[q], q)
        some = adj_recv.at[q, pl.ds(0, m - 1)]
        pltpu.make_async_copy(some, some, rs_send.at[q]).wait()
    left(meta_recv, META)
    left(src_mid, SRC1)
    left(src_recv, SRC2)
    left(mis_recv, MIS)


def per_device(n, m, records, virtual_sources, pair_group, pair_receiver, pair_source, observed):
    chans, time_len = records.shape
    pairs, width = observed.shape
    bins = width // 2
    chunks = max(1, bins // 256)
    part = bins // chunks
    rows_out = chans // m
    sources = virtual_sources.shape[0]
    rows = 2 * n * CAP
    group_row = pair_group.reshape(1, pairs)
    group_col = pair_group.reshape(pairs, 1)
    adjoint, misfit = pl.pallas_call(
        functools.partial(kernel, n, m, chunks),
        out_shape=(
            jax.ShapeDtypeStruct((rows_out, time_len), F32),
            jax.ShapeDtypeStruct((1, pairs), F32),
        ),
        in_specs=[pl.BlockSpec(memory_space=pltpu.VMEM)] * 7,
        out_specs=(pl.BlockSpec(memory_space=pltpu.VMEM),) * 2,
        scratch_shapes=[
            pltpu.VMEM((chunks, n, 8, part), F32),
            pltpu.VMEM((chunks, n, 8, part), F32),
            pltpu.VMEM((n, 1, 128), F32),
            pltpu.VMEM((n, 1, 128), F32),
            pltpu.VMEM((n, 4, 128), F32),
            pltpu.VMEM((n, 4, 128), F32),
            pltpu.VMEM((4, 128), F32),
            pltpu.VMEM((n, 4, 128), F32),
            pltpu.VMEM((chunks, m, 2 * rows_out, part), F32),
            pltpu.VMEM((chunks, m, 2 * rows_out, part), F32),
            pltpu.VMEM((n, 1, 128), F32),
            pltpu.VMEM((n, 1, 128), F32),
            pltpu.VMEM((time_len, width), BF16),
            pltpu.VMEM((time_len // STEP, 1, bins), F32),
            pltpu.VMEM((time_len // STEP, 1, bins), F32),
            pltpu.VMEM((STEP, bins), F32),
            pltpu.VMEM((STEP, bins), F32),
            pltpu.VMEM((chans, width), F32),
            pltpu.VMEM((chunks, 2 * chans, part), BF16),
            pltpu.VMEM((chunks, 2 * chans, part), BF16),
            pltpu.VMEM((rows, 2 * chans), BF16),
            pltpu.VMEM((rows, 2 * chans), BF16),
            pltpu.VMEM((2 * chans, rows), BF16),
            pltpu.VMEM((2 * chans, rows), BF16),
            pltpu.VMEM((rows, sources), BF16),
            pltpu.VMEM((rows, 128), F32),
            pltpu.SemaphoreType.DMA((chunks + 4,)),
            pltpu.SemaphoreType.DMA((chunks + 4,)),
            pltpu.SemaphoreType.DMA((chunks,)),
            pltpu.SemaphoreType.DMA((chunks,)),
        ],
        compiler_params=pltpu.CompilerParams(
            collective_id=0, has_side_effects=True, vmem_limit_bytes=56 * 1024 * 1024
        ),
    )(
        records,
        virtual_sources.reshape(sources, 1),
        group_row,
        group_col,
        pair_receiver.reshape(1, pairs),
        pair_source.reshape(1, pairs),
        observed,
    )
    return adjoint, misfit.reshape(pairs)


def solution(mesh):
    return jax.shard_map(
        functools.partial(per_device, mesh.shape["chan"], mesh.shape["src"]),
        mesh=mesh,
        in_specs=(
            P("chan", None),
            P("src"),
            P(("chan", "src"), None),
            P(("chan", "src")),
            P(("chan", "src")),
            P(("chan", "src"), None),
        ),
        out_specs=(P(("chan", "src"), None), P(("chan", "src"))),
        check_vma=False,
    )
```

time: 527 us -> 87.4 us (0.17)
  waiting for transfers between devices: 263 us -> 0 us
  other arithmetic: 151 us -> 0 us
  Pallas kernels: 0 us -> 82.1 us
  matrix products: 42.2 us -> 0 us
  starting transfers between devices: 30.3 us -> 0 us
  local copies, waits for them, and re-layouts: 24.8 us -> 4.45 us
  between operations: 14.3 us -> 0.66 us
    psum x1 -> x0, waiting for transfers between devices: 184 us -> none  [per_device(): sources = lax.psum(picked, 'chan')]
    pallas_call x0 -> x1, Pallas kernels: none -> 82.1 us  [per_device(): pl.pallas_call(functools.partial(kernel, n, m, chunks), out_shape=(jax.Sh...]
    another operation x9 -> x0, other arithmetic: 72.4 us -> none
    cos x8 -> x0, other arithmetic: 66.4 us -> none  [fourier_basis(): return jnp.concatenate([jnp.cos(angles), -jnp.sin(angles)], axis=1)]
    all_to_all x3 -> x0, waiting for transfers between devices: 51.1 us -> none  [the longest x1 51.1 us: per_device(): lax.all_to_all(send_terms, 'chan', split_axis=0, concat_axis=0, tiled=True)]
    dot_general x17 -> x0, matrix products: 42.2 us -> none  [the longest x8 27.4 us: fill_block(): lax.dot_general(spectral, fourier_table, (((1,), (1,)), ((), ())), precis...]
    all_to_all x3 -> x0, starting transfers between devices: 30.2 us -> none  [the longest x1 13 us: per_device(): lax.all_to_all(send_receiver, 'chan', split_axis=0, concat_axis=0, tiled=...]
    reduce_scatter x1 -> x0, waiting for transfers between devices: 28.4 us -> none  [per_device(): lax.psum_scatter(inverse(adjoint_spectra, time_len), 'src', scatter_dimen...]
  transfers between devices with their start and end apart: 5 -> 0, of which waited for: 3 -> 0; matrix products, arithmetic and copies ran while one was open for 17% -> 0% of each run, Pallas kernels for 0% -> 0%
where the time goes in v1:
time: 87.4 us; the launch traced here: 87.3 us
  Pallas kernels  82.1 us (94%)
  local copies, waits for them, and re-layouts  4.45 us (5%)
    pallas_call x1, Pallas kernels, per_device(): pl.pallas_call(functools.partial(kernel, n, m, chunks), out_shape=(jax.Sh...  82.1 us
    unnamed x9, local copies, waits for them, and re-layouts  3.78 us

profile of v1, /device:TPU:1, one launch (start us, length us, event | category | flops | bytes accessed | tf_op | source)
XLA Modules:
  0.0 87.3 jit_solution(9522650927780150297)
XLA Ops:
  0.6 0.0 copy-start.1
  0.6 0.6 copy-done.1
  1.3 0.0 copy-start
  1.3 0.7 copy.8.vs_ref
  2.0 0.0 copy-done
  2.0 0.7 copy.9.gcol_ref
  2.7 82.1 %shard_map.77 = (f32[32,4096]{1,0:T(8,128)}, f32[1,128]{1,0:T(1,128)}) custom-call(bf16[128,4096]{1,0:T(8,128)(2,1)} %rec_ref.1, s32[16,1]{1,0:T(8,128)} %copy.8.vs_ref, s32[1,128]{1,0:T(1,128)} %bitcast.5, s32[128,1]{1,0:T(8,128)} %copy.9.gcol_ref, s32[1,128]{1,0:T(1,128)} %bitcast.6, s32[1,128]{1,0:T(1,128)} %bitcast.7, f32[128,2048]{1,0:T(8,128)} %obs_ref.1), custom_call_target="tpu_custom_call" | custom-call | tf_op jit(solution)/shard_map/pallas_call | solution.py:372
  84.9 0.0 copy-start.2
  84.9 1.9 %copy.12 = f32[32,4096]{1,0:T(8,128)} copy(f32[32,4096]{1,0:T(8,128)} %get-tuple-element.8) | data formatting | bytes 1048576
  86.7 0.0 copy-done.2
  86.7 0.5 copy.13
Async XLA Ops:
  0.6 0.7 copy-start.1
  1.3 0.7 copy-start
  84.9 1.9 %copy-start.2 = (f32[1,128]{1,0:T(1,128)S(1)}, f32[1,128]{1,0:T(1,128)}, u32[]{:S(2)}) copy-start(f32[1,128]{1,0:T(1,128)} %get-tuple-element.5) | copy-start | bytes 1540

commit v2 on v0

v2 whole, which is shorter than its diff:
```python
import functools
import math

import jax
import jax.numpy as jnp
from jax import lax
from jax.experimental import pallas as pl
from jax.experimental.pallas import tpu as pltpu
from jax.sharding import PartitionSpec as P

K0 = 64
CAP = 4
STEP = 64
PART = 128
MESH = pl.DeviceIdType.MESH
F32 = jnp.float32
BF16 = jnp.bfloat16


def iota(shape, axis):
    return lax.broadcasted_iota(jnp.int32, shape, axis)


def ones_where(mask):
    return jnp.where(mask, 1.0, 0.0)


def one_hot(mask):
    return ones_where(mask).astype(BF16)


def dot(left, right):
    return jnp.dot(left, right, preferred_element_type=F32)


def dot_t(left, right):
    return lax.dot_general(left, right, (((1,), (1,)), ((), ())), preferred_element_type=F32)


def halves(value):
    high = value.astype(BF16)
    return high, (value - high.astype(F32)).astype(BF16)


def dot2(left, pair):
    return dot(left, pair[0]) + dot(left, pair[1])


def lanes_of(values, lane):
    return jnp.sum(jnp.where(iota(values.shape, 1) == lane, values, 0.0), axis=1, keepdims=True)


def kernel(
    nz,
    np_,
    m,
    room,
    rec_ref,
    vs_ref,
    group_ref,
    prec_ref,
    psrc_ref,
    obs_ref,
    out_ref,
    mis_ref,
    over_ref,
    z_send,
    z_recv,
    x_send,
    x_recv,
    zmeta_send,
    zmeta_recv,
    xmeta_send,
    xmeta_recv,
    src_send,
    src_mid,
    src_part,
    src_line,
    src_all,
    src_recv,
    adj_send,
    adj_recv,
    xmis_send,
    xmis_recv,
    zmis_send,
    zmis_recv,
    flag_send,
    flag_recv,
    table,
    cos_a,
    sin_a,
    cos_b,
    sin_b,
    spec,
    white_hi,
    white_lo,
    perm_ref,
    g_ref,
    gt_ref,
    h_ref,
    mis_acc,
    zs_sem,
    zr_sem,
    xs_sem,
    xr_sem,
    ys_sem,
    yr_sem,
    small_s,
    small_r,
):
    chans, time_len = rec_ref.shape
    pairs, width = obs_ref.shape
    bins = width // 2
    chunks = bins // PART
    rows_out = chans // m
    sources = vs_ref.shape[1]
    z_rows = nz * room
    plane_slots = nz * CAP
    slots = np_ * plane_slots
    me = lax.axis_index("chan")
    owner = lax.axis_index("src")
    my_z = lax.rem(me // 2, nz)
    my_p = (me // (2 * nz)) * 2 + lax.rem(me, 2)

    def on_line(z):
        return {"chan": (me // (2 * nz)) * (2 * nz) + z * 2 + lax.rem(me, 2)}

    def in_plane(p):
        return {"chan": (p // 2) * (2 * nz) + my_z * 2 + lax.rem(p, 2)}

    def in_column(y):
        return {"src": y}

    barrier = pltpu.get_barrier_semaphore()

    def greet(size, mine, where):
        def one(i, carry):
            pl.semaphore_signal(
                barrier, inc=1, device_id=where(lax.rem(mine + i, size)), device_id_type=MESH
            )
            return carry

        lax.fori_loop(1, size, one, 0)

    greet(nz, my_z, on_line)
    greet(np_, my_p, in_plane)
    greet(m, owner, in_column)

    def spread(size, mine, where, send, recv, send_sem, recv_sem):
        def one(i, carry):
            other = lax.rem(mine + i, size)
            pltpu.make_async_remote_copy(
                src_ref=send(other),
                dst_ref=recv.at[mine],
                send_sem=send_sem,
                recv_sem=recv_sem,
                device_id=where(other),
                device_id_type=MESH,
            ).start()
            return carry

        pltpu.make_async_copy(send(mine), recv.at[mine], recv_sem).start()
        lax.fori_loop(1, size, one, 0)

    def arrived(recv, sem):
        pltpu.make_async_copy(recv, recv, sem).wait()

    def left(recv, sem):
        some = recv.at[pl.ds(0, recv.shape[0] - 1)]
        pltpu.make_async_copy(some, some, sem).wait()

    def spread_z(send, recv, send_sem, recv_sem):
        spread(nz, my_z, on_line, send, recv, send_sem, recv_sem)

    def spread_x(send, recv, send_sem, recv_sem):
        spread(np_, my_p, in_plane, send, recv, send_sem, recv_sem)

    ZMETA, XMETA, SRC1, SRC2, SRC3, XMIS, ZMIS, FLAG = range(8)

    diagonal = iota((pairs, pairs), 0) == iota((pairs, pairs), 1)
    earlier = iota((pairs, pairs), 0) < iota((pairs, pairs), 1)
    group = group_ref[...]
    group_col = jnp.sum(jnp.where(diagonal, group, 0), axis=1, keepdims=True)
    rank = jnp.sum(jnp.where((group_col == group) & earlier, 1, 0), axis=0, keepdims=True)
    slab = lax.rem(group >> 1, nz)
    slab_col = lax.rem(group_col >> 1, nz)
    place = jnp.sum(jnp.where((slab_col == slab) & earlier, 1, 0), axis=0, keepdims=True)
    plane = lax.div(group, 2 * nz) * 2 + (group & 1)
    over = jnp.max(jnp.where(place >= room, 1.0, 0.0), axis=1, keepdims=True)
    row = jnp.where(place < room, slab * room + place, -1)
    pick = ones_where(row == iota((z_rows, pairs), 0))
    pick_bf = pick.astype(BF16)

    def pack(q):
        block = jnp.concatenate(
            [
                obs_ref[:, q * PART : (q + 1) * PART],
                obs_ref[:, bins + q * PART : bins + (q + 1) * PART],
            ],
            axis=1,
        )
        values = dot2(pick_bf, halves(block))
        z_send[q, :, 0:room, :] = values[:, :PART].reshape(nz, room, PART)
        z_send[q, :, room : 2 * room, :] = values[:, PART:].reshape(nz, room, PART)

    def send_z(q):
        spread_z(lambda z: z_send.at[q, z], z_recv.at[q], zs_sem.at[q], zr_sem.at[q])

    pack(0)
    lane_z = iota((z_rows, 128), 1)
    rank_z = lax.rem(iota((z_rows, 128), 0), room)

    def along(values):
        return jnp.sum(jnp.where(pick > 0.5, values.astype(F32), 0.0), axis=1, keepdims=True)

    coded = (
        jnp.where(lane_z == rank_z, along(plane * CAP + rank + 1), 0.0)
        + jnp.where(lane_z == rank_z + 32, along(prec_ref[...]), 0.0)
        + jnp.where(lane_z == rank_z + 64, along(psrc_ref[...]), 0.0)
    )
    fold_z = one_hot(
        iota((nz, z_rows), 0) == lax.div(iota((nz, z_rows), 1), room)
    )
    zmeta = dot(fold_z, coded.astype(BF16)) + jnp.where(iota((nz, 128), 1) == 100, over, 0.0)
    zmeta_send[...] = zmeta.reshape(nz, 1, 128)

    pl.semaphore_wait(barrier, nz - 1 + np_ - 1 + m - 1)

    spread_z(lambda z: zmeta_send.at[z], zmeta_recv, small_s.at[ZMETA], small_r.at[ZMETA])
    send_z(0)
    first = min(4, chunks)
    for q in range(1, first):
        pack(q)
        send_z(q)
    for q in range(first, chunks):
        pack(q)

    unit = math.pi / time_len
    steps = time_len // STEP
    phase_b = ((K0 + iota((STEP, bins), 1)) * iota((STEP, bins), 0)) & (2 * time_len - 1)
    angle_b = phase_b.astype(F32) * unit
    cos_b[...] = jnp.cos(angle_b)
    sin_b[...] = jnp.sin(angle_b)
    phase_a = ((K0 + iota((steps, bins), 1)) * (iota((steps, bins), 0) * STEP)) & (2 * time_len - 1)
    angle_a = phase_a.astype(F32) * unit
    cos_a[...] = jnp.cos(angle_a).reshape(steps, 1, bins)
    sin_a[...] = jnp.sin(angle_a).reshape(steps, 1, bins)

    def fill(i, carry):
        at = pl.ds(pl.multiple_of(i * STEP, STEP), STEP)
        for q in range(chunks):
            part = slice(q * PART, (q + 1) * PART)
            ca, sa = cos_a[i, :, part], sin_a[i, :, part]
            cb, sb = cos_b[:, part], sin_b[:, part]
            table[at, 2 * q * PART : (2 * q + 1) * PART] = (ca * cb - sa * sb).astype(BF16)
            table[at, (2 * q + 1) * PART : (2 * q + 2) * PART] = (-(sa * cb) - ca * sb).astype(BF16)
        return carry

    lax.fori_loop(0, steps, fill, 0)

    def transform(i, power):
        at = pl.ds(pl.multiple_of(i * 2 * PART, 2 * PART), 2 * PART)
        values = dot(rec_ref[...], table[:, at])
        spec[:, at] = values
        return power + jnp.sum(values * values, axis=1, keepdims=True)

    power = lax.fori_loop(0, chunks, transform, jnp.zeros((chans, 1), F32))
    norm = jnp.sqrt(power / bins + 1e-6)

    wanted = jnp.sum(
        jnp.where(iota((sources, sources), 0) == iota((sources, sources), 1), vs_ref[...], 0),
        axis=1,
        keepdims=True,
    )
    chosen = one_hot(iota((sources, chans), 1) == wanted - me * chans)
    for q in range(chunks):
        pair = halves(spec[:, 2 * q * PART : (2 * q + 2) * PART] / norm)
        white_hi[q], white_lo[q] = pair
        src_send[q] = dot2(chosen, pair)
    spread_x(lambda p: src_send.at[p], src_mid, small_s.at[SRC1], small_r.at[SRC1])

    arrived(zmeta_recv, small_r.at[ZMETA])
    unfold_z = one_hot(lax.div(iota((z_rows, nz), 0), room) == iota((z_rows, nz), 1))
    metas = zmeta_recv[...].reshape(nz, 128)
    line_over = jnp.max(jnp.where(iota((nz, 128), 1) == 100, metas, 0.0), keepdims=True)
    wide = dot(unfold_z, metas.astype(BF16))
    code = lanes_of(wide, rank_z).astype(jnp.int32) - 1
    came_from = lax.div(iota((z_rows, 1), 0), room)
    to_plane = jnp.where(code >= 0, code >> 2, -1)
    within = came_from * CAP + (code & 3)
    target = jnp.where(code >= 0, to_plane * plane_slots + within, -1)
    perm_ref[...] = ones_where(iota((z_rows, slots), 1) == target).T.astype(BF16)
    to_plane_hot = ones_where(iota((z_rows, 128), 1) == to_plane)
    coded = jnp.where(lane_z == within, lanes_of(wide, rank_z + 32) + 1.0, 0.0) + jnp.where(
        lane_z == within + plane_slots, lanes_of(wide, rank_z + 64), 0.0
    )
    xmeta = dot(to_plane_hot.T[:np_].astype(BF16), coded.astype(BF16)) + jnp.where(
        iota((np_, 128), 1) == 100, line_over, 0.0
    )
    xmeta_send[...] = xmeta.reshape(np_, 1, 128)
    spread_x(lambda p: xmeta_send.at[p], xmeta_recv, small_s.at[XMETA], small_r.at[XMETA])

    def forward_x(q):
        arrived(z_recv.at[q], zr_sem.at[q])
        block = jnp.concatenate(
            [
                z_recv[q, :, 0:room, :].reshape(z_rows, PART),
                z_recv[q, :, room : 2 * room, :].reshape(z_rows, PART),
            ],
            axis=1,
        )
        values = dot2(perm_ref[...], halves(block))
        x_send[q, :, 0:plane_slots, :] = values[:, :PART].reshape(np_, plane_slots, PART)
        x_send[q, :, plane_slots : 2 * plane_slots, :] = values[:, PART:].reshape(
            np_, plane_slots, PART
        )
        spread_x(lambda p: x_send.at[q, p], x_recv.at[q], xs_sem.at[q], xr_sem.at[q])

    forward_x(0)

    arrived(src_mid, small_r.at[SRC1])
    src_part[...] = jnp.sum(src_mid[...], axis=0)
    spread_z(lambda z: src_part, src_line, small_s.at[SRC2], small_r.at[SRC2])
    second = min(6, chunks)
    for q in range(first, second):
        send_z(q)
    for q in range(1, first):
        forward_x(q)

    arrived(xmeta_recv, small_r.at[XMETA])
    unfold_x = one_hot(lax.div(iota((slots, np_), 0), plane_slots) == iota((slots, np_), 1))
    metas = xmeta_recv[...].reshape(np_, 128)
    flag_send[...] = jnp.broadcast_to(
        jnp.max(jnp.where(iota((np_, 128), 1) == 100, metas, 0.0), keepdims=True), (1, 128)
    )
    spread(m, owner, in_column, lambda y: flag_send, flag_recv, small_s.at[FLAG], small_r.at[FLAG])
    wide = dot(unfold_x, metas.astype(BF16))
    lane_x = lax.rem(iota((slots, 128), 0), plane_slots)
    receiver = lanes_of(wide, lane_x).astype(jnp.int32) - 1
    source = lanes_of(wide, lane_x + plane_slots).astype(jnp.int32)
    hits = ones_where(iota((slots, chans), 1) == receiver)
    g_ref[...] = hits.astype(BF16)
    gt_ref[...] = hits.T.astype(BF16)
    h_ref[...] = one_hot((iota((slots, sources), 1) == source) & (receiver >= 0))

    arrived(src_line, small_r.at[SRC2])
    src_all[...] = jnp.sum(src_line[...], axis=0)
    spread_x(lambda p: src_all, src_recv, small_s.at[SRC3], small_r.at[SRC3])
    for q in range(second, chunks):
        send_z(q)
    arrived(src_recv, small_r.at[SRC3])

    mis_acc[...] = jnp.zeros_like(mis_acc)

    def correlate(q):
        arrived(x_recv.at[q], xr_sem.at[q])
        band = (q * PART + iota((1, PART), 1)).astype(F32)
        taper = 0.5 - 0.5 * jnp.cos((band + 0.5) * (2.0 * math.pi / bins))
        source_rows = dot2(h_ref[...], halves(src_recv[q]))
        receiver_rows = dot2(g_ref[...], (white_hi[q], white_lo[q]))
        s_re, s_im = source_rows[:, :PART], source_rows[:, PART:]
        r_re, r_im = receiver_rows[:, :PART], receiver_rows[:, PART:]
        d_re = s_re * r_re + s_im * r_im - x_recv[q, :, 0:plane_slots, :].reshape(slots, PART)
        d_im = s_re * r_im - s_im * r_re - x_recv[q, :, plane_slots : 2 * plane_slots, :].reshape(
            slots, PART
        )
        e_re, e_im = taper * d_re, taper * d_im
        mis_acc[...] += e_re * d_re + e_im * d_im
        terms = jnp.concatenate([e_re * s_re - e_im * s_im, e_re * s_im + e_im * s_re], axis=1)
        adj_send[q] = dot2(gt_ref[...], halves(terms)).reshape(m, rows_out, 2 * PART)
        spread(
            m,
            owner,
            in_column,
            lambda y: adj_send.at[q, y],
            adj_recv.at[q],
            ys_sem.at[q],
            yr_sem.at[q],
        )

    def inverse(q):
        arrived(adj_recv.at[q], yr_sem.at[q])
        total = adj_recv[q, 0]
        for y in range(1, m):
            total = total + adj_recv[q, y]
        high, low = halves(total * (1.0 / math.sqrt(bins)))
        both = jnp.concatenate([high, low], axis=0)
        span = min(512, time_len)

        def one(i, carry):
            at = pl.ds(pl.multiple_of(i * span, span), span)
            product = dot_t(both, table[at, 2 * q * PART : (2 * q + 2) * PART])
            values = product[:rows_out] + product[rows_out:]
            if q == 0:
                out_ref[:, at] = values
            else:
                out_ref[:, at] += values
            return carry

        lax.fori_loop(0, time_len // span, one, 0)

    for q in range(chunks):
        correlate(q)
        if q + first < chunks:
            forward_x(q + first)
        if q >= 2 and q < chunks - 1:
            inverse(q - 2)

    total = jnp.sum(mis_acc[...], axis=1, keepdims=True) * (0.5 / bins)
    fold_x = one_hot(iota((np_, slots), 0) == lax.div(iota((np_, slots), 1), plane_slots))
    spread_out = jnp.where(iota((slots, 128), 1) == lane_x, total, 0.0)
    xmis_send[...] = dot2(fold_x, halves(spread_out)).reshape(np_, 1, 128)
    spread_x(lambda p: xmis_send.at[p], xmis_recv, small_s.at[XMIS], small_r.at[XMIS])

    for q in range(max(0, chunks - 3), chunks - 1):
        inverse(q)

    arrived(xmis_recv, small_r.at[XMIS])
    back = dot2(to_plane_hot[:, :np_].astype(BF16), halves(xmis_recv[...].reshape(np_, 128)))
    spread_out = jnp.where(lane_z == rank_z, lanes_of(back, within), 0.0)
    zmis_send[...] = dot2(fold_z, halves(spread_out)).reshape(nz, 1, 128)
    spread_z(lambda z: zmis_send.at[z], zmis_recv, small_s.at[ZMIS], small_r.at[ZMIS])

    inverse(chunks - 1)

    arrived(zmis_recv, small_r.at[ZMIS])
    back = dot2(unfold_z, halves(zmis_recv[...].reshape(nz, 128)))
    mis_ref[...] = jnp.sum(pick * lanes_of(back, rank_z), axis=0, keepdims=True)
    arrived(flag_recv, small_r.at[FLAG])
    over_ref[...] = jnp.max(flag_recv[...], axis=0)

    for q in range(chunks):
        left(z_recv.at[q], zs_sem.at[q])
        left(x_recv.at[q], xs_sem.at[q])
        left(adj_recv.at[q], ys_sem.at[q])
    for recv, sem in (
        (zmeta_recv, ZMETA),
        (xmeta_recv, XMETA),
        (src_mid, SRC1),
        (src_line, SRC2),
        (src_recv, SRC3),
        (xmis_recv, XMIS),
        (zmis_recv, ZMIS),
        (flag_recv, FLAG),
    ):
        left(recv, small_s.at[sem])


def exchange(nz, np_, m, room, number, operands):
    records, observed = operands[0], operands[5]
    chans, time_len = records.shape
    pairs, width = observed.shape
    bins = width // 2
    chunks = bins // PART
    rows_out = chans // m
    sources = operands[1].shape[1]
    slots = np_ * nz * CAP
    assert chunks == np_
    vmem = pltpu.VMEM
    return pl.pallas_call(
        functools.partial(kernel, nz, np_, m, room),
        out_shape=(
            jax.ShapeDtypeStruct((rows_out, time_len), F32),
            jax.ShapeDtypeStruct((1, pairs), F32),
            jax.ShapeDtypeStruct((1, 128), F32),
        ),
        in_specs=[pl.BlockSpec(memory_space=vmem)] * 6,
        out_specs=(pl.BlockSpec(memory_space=vmem),) * 3,
        scratch_shapes=[
            vmem((chunks, nz, 2 * room, PART), F32),
            vmem((chunks, nz, 2 * room, PART), F32),
            vmem((chunks, np_, 2 * nz * CAP, PART), F32),
            vmem((chunks, np_, 2 * nz * CAP, PART), F32),
            vmem((nz, 1, 128), F32),
            vmem((nz, 1, 128), F32),
            vmem((np_, 1, 128), F32),
            vmem((np_, 1, 128), F32),
            vmem((np_, sources, 2 * PART), F32),
            vmem((np_, sources, 2 * PART), F32),
            vmem((sources, 2 * PART), F32),
            vmem((nz, sources, 2 * PART), F32),
            vmem((sources, 2 * PART), F32),
            vmem((np_, sources, 2 * PART), F32),
            vmem((chunks, m, rows_out, 2 * PART), F32),
            vmem((chunks, m, rows_out, 2 * PART), F32),
            vmem((np_, 1, 128), F32),
            vmem((np_, 1, 128), F32),
            vmem((nz, 1, 128), F32),
            vmem((nz, 1, 128), F32),
            vmem((1, 128), F32),
            vmem((m, 1, 128), F32),
            vmem((time_len, width), BF16),
            vmem((time_len // STEP, 1, bins), F32),
            vmem((time_len // STEP, 1, bins), F32),
            vmem((STEP, bins), F32),
            vmem((STEP, bins), F32),
            vmem((chans, width), F32),
            vmem((chunks, chans, 2 * PART), BF16),
            vmem((chunks, chans, 2 * PART), BF16),
            vmem((slots, nz * room), BF16),
            vmem((slots, chans), BF16),
            vmem((chans, slots), BF16),
            vmem((slots, sources), BF16),
            vmem((slots, PART), F32),
            pltpu.SemaphoreType.DMA((chunks,)),
            pltpu.SemaphoreType.DMA((chunks,)),
            pltpu.SemaphoreType.DMA((chunks,)),
            pltpu.SemaphoreType.DMA((chunks,)),
            pltpu.SemaphoreType.DMA((chunks,)),
            pltpu.SemaphoreType.DMA((chunks,)),
            pltpu.SemaphoreType.DMA((8,)),
            pltpu.SemaphoreType.DMA((8,)),
        ],
        compiler_params=pltpu.CompilerParams(
            collective_id=number, has_side_effects=True, vmem_limit_bytes=56 * 1024 * 1024
        ),
    )(*operands)


def per_device(n, m, records, virtual_sources, pair_group, pair_receiver, pair_source, observed):
    pairs, width = observed.shape
    np_ = width // 2 // PART
    nz = n // np_
    most = np_ * CAP
    usual = max(8, most * 3 // 4 // 8 * 8)
    operands = (
        records,
        virtual_sources.reshape(1, -1),
        pair_group.reshape(1, pairs),
        pair_receiver.reshape(1, pairs),
        pair_source.reshape(1, pairs),
        observed,
    )
    adjoint, misfit, over = exchange(nz, np_, m, usual, 0, operands)
    adjoint, misfit = lax.cond(
        over[0, 0] > 0.0,
        lambda held: exchange(nz, np_, m, most, 1, operands)[:2],
        lambda held: held,
        (adjoint, misfit),
    )
    return adjoint, misfit.reshape(pairs)


def solution(mesh):
    return jax.shard_map(
        functools.partial(per_device, mesh.shape["chan"], mesh.shape["src"]),
        mesh=mesh,
        in_specs=(
            P("chan", None),
            P("src"),
            P(("chan", "src"), None),
            P(("chan", "src")),
            P(("chan", "src")),
            P(("chan", "src"), None),
        ),
        out_specs=(P(("chan", "src"), None), P(("chan", "src"))),
        check_vma=False,
    )
```

time: 527 us -> 76.3 us (0.14)
  waiting for transfers between devices: 263 us -> 0 us
  other arithmetic: 151 us -> 0 us
  Pallas kernels: 0 us -> 72.5 us
  matrix products: 42.2 us -> 0 us
  starting transfers between devices: 30.3 us -> 0 us
  local copies, waits for them, and re-layouts: 24.8 us -> 2.64 us
  between operations: 14.3 us -> 0.75 us
    psum x1 -> x0, waiting for transfers between devices: 184 us -> none  [per_device(): sources = lax.psum(picked, 'chan')]
    pallas_call x0 -> x1, Pallas kernels: none -> 72.5 us  [exchange(): pl.pallas_call(functools.partial(kernel, nz, np_, m, room), out_shape=(ja...]
    another operation x9 -> x0, other arithmetic: 72.4 us -> none
    cos x8 -> x0, other arithmetic: 66.4 us -> none  [fourier_basis(): return jnp.concatenate([jnp.cos(angles), -jnp.sin(angles)], axis=1)]
    all_to_all x3 -> x0, waiting for transfers between devices: 51.1 us -> none  [the longest x1 51.1 us: per_device(): lax.all_to_all(send_terms, 'chan', split_axis=0, concat_axis=0, tiled=True)]
    dot_general x17 -> x0, matrix products: 42.2 us -> none  [the longest x8 27.4 us: fill_block(): lax.dot_general(spectral, fourier_table, (((1,), (1,)), ((), ())), precis...]
    all_to_all x3 -> x0, starting transfers between devices: 30.2 us -> none  [the longest x1 13 us: per_device(): lax.all_to_all(send_receiver, 'chan', split_axis=0, concat_axis=0, tiled=...]
    reduce_scatter x1 -> x0, waiting for transfers between devices: 28.4 us -> none  [per_device(): lax.psum_scatter(inverse(adjoint_spectra, time_len), 'src', scatter_dimen...]
  transfers between devices with their start and end apart: 5 -> 0, of which waited for: 3 -> 0; matrix products, arithmetic and copies ran while one was open for 17% -> 0% of each run, Pallas kernels for 0% -> 0%
where the time goes in v2:
time: 76.3 us; the launch traced here: 76 us
  Pallas kernels  72.5 us (95%)
  local copies, waits for them, and re-layouts  2.64 us (3%)
    pallas_call x1, Pallas kernels, exchange(): pl.pallas_call(functools.partial(kernel, nz, np_, m, room), out_shape=(ja...  72.5 us
    unnamed x16, local copies, waits for them, and re-layouts  2.64 us

profile of v2, /device:TPU:1, one launch (start us, length us, event | category | flops | bytes accessed | tf_op | source)
XLA Modules:
  0.0 76.0 jit_solution(11144063788669752689)
XLA Ops:
  0.6 0.0 copy-start.5
  0.6 0.0 copy-start.2
  0.7 0.0 copy-start.3
  0.7 0.0 copy-start.4
  0.7 0.6 copy-done.5
  1.3 0.0 copy-done.2
  1.3 0.0 copy-done.3
  1.3 0.0 copy-done.4
  1.3 0.0 copy-start
  1.3 0.0 copy-start.1
  1.3 72.5 %shard_map.77 = (f32[32,4096]{1,0:T(8,128)S(1)}, f32[1,128]{1,0:T(1,128)S(1)}, f32[1,128]{1,0:T(1,128)}) custom-call(bf16[128,4096]{1,0:T(8,128)(2,1)} %rec_ref.1, s32[1,16]{1,0:T(1,128)S(1)} %bitcast.7, s32[1,128]{1,0:T(1,128)S(1)} %bitcast.9, s32[1,128]{1,0:T(1,128)S(1)} %bitcast.11, s32[1,128]{1,0:T(1,128)S(1)} %bitcast.13, f32[128,2048]{1,0:T(8,128)} %obs_ref.1), custom_call_target="tpu_custom_call" | custom-call | tf_op jit(solution)/shard_map/pallas_call | solution.py:460
  73.8 0.0 copy-start.6
  73.8 0.7 copy-done.6
  74.5 0.0 copy-done
  74.5 0.0 copy-done.1
  74.5 0.2 conditional.1
  74.7 0.8 %copy.14 = f32[32,4096]{1,0:T(8,128)} copy(f32[32,4096]{1,0:T(8,128)S(1)} %get-tuple-element.45) | data formatting | bytes 1048576
  75.5 0.5 copy.15
Async XLA Ops:
  0.6 0.7 copy-start.5
  0.6 0.7 copy-start.2
  0.7 0.7 copy-start.3
  0.7 0.7 copy-start.4
  1.3 73.2 %copy-start = (bf16[128,4096]{1,0:T(8,128)(2,1)S(1)}, bf16[128,4096]{1,0:T(8,128)(2,1)}, u32[]{:S(2)}) copy-start(bf16[128,4096]{1,0:T(8,128)(2,1)} %rec_ref.1) | copy-start | bytes 3145732
  1.3 73.2 %copy-start.1 = (f32[128,2048]{1,0:T(8,128)S(1)}, f32[128,2048]{1,0:T(8,128)}, u32[]{:S(2)}) copy-start(f32[128,2048]{1,0:T(8,128)} %obs_ref.1) | copy-start | bytes 3145732
  73.8 0.7 copy-start.6

commit v3 on v2

--- a/solution.py
+++ b/solution.py
@@ -76,17 +76,17 @@
     src_mid,
     src_part,
     src_line,
+    src_own,
+    src_rows,
     src_all,
     src_recv,
     adj_send,
     adj_recv,
-    xmis_send,
-    xmis_recv,
-    zmis_send,
-    zmis_recv,
+    mis_send,
+    mis_recv,
     flag_send,
     flag_recv,
-    table,
+    tables,
     cos_a,
     sin_a,
     cos_b,
@@ -119,48 +119,37 @@
     slots = np_ * plane_slots
     me = lax.axis_index("chan")
     owner = lax.axis_index("src")
-    my_z = lax.rem(me // 2, nz)
-    my_p = (me // (2 * nz)) * 2 + lax.rem(me, 2)
-
-    def on_line(z):
-        return {"chan": (me // (2 * nz)) * (2 * nz) + z * 2 + lax.rem(me, 2)}
-
-    def in_plane(p):
-        return {"chan": (p // 2) * (2 * nz) + my_z * 2 + lax.rem(p, 2)}
-
-    def in_column(y):
-        return {"src": y}
+    my_z = lax.rem(lax.div(me, 2), nz)
+    my_p = lax.div(me, 2 * nz) * 2 + lax.rem(me, 2)
+    line = [lax.rem(my_z + i, nz) for i in range(nz)]
+    plane_ids = [lax.rem(my_p + i, np_) for i in range(np_)]
+    owners = [lax.rem(owner + i, m) for i in range(m)]
+    base = [lax.div(p, 2) * (2 * nz) + lax.rem(p, 2) for p in plane_ids]
+
+    def there(i, j):
+        return {"chan": base[i] + 2 * line[j]}
+
+    on_line = [there(0, j) for j in range(nz)]
+    in_plane = [there(i, 0) for i in range(np_)]
+    in_column = [{"src": y} for y in owners]
 
     barrier = pltpu.get_barrier_semaphore()
-
-    def greet(size, mine, where):
-        def one(i, carry):
-            pl.semaphore_signal(
-                barrier, inc=1, device_id=where(lax.rem(mine + i, size)), device_id_type=MESH
-            )
-            return carry
-
-        lax.fori_loop(1, size, one, 0)
-
-    greet(nz, my_z, on_line)
-    greet(np_, my_p, in_plane)
-    greet(m, owner, in_column)
-
-    def spread(size, mine, where, send, recv, send_sem, recv_sem):
-        def one(i, carry):
-            other = lax.rem(mine + i, size)
+    for devices in (on_line, in_plane, in_column):
+        for device in devices[1:]:
+            pl.semaphore_signal(barrier, inc=1, device_id=device, device_id_type=MESH)
+
+    def spread(places, devices, send, recv, send_sem, recv_sem):
+        mine = places[0]
+        for place, device in zip(places[1:], devices[1:]):
             pltpu.make_async_remote_copy(
-                src_ref=send(other),
+                src_ref=send(place),
                 dst_ref=recv.at[mine],
                 send_sem=send_sem,
                 recv_sem=recv_sem,
-                device_id=where(other),
+                device_id=device,
                 device_id_type=MESH,
             ).start()
-            return carry
-
         pltpu.make_async_copy(send(mine), recv.at[mine], recv_sem).start()
-        lax.fori_loop(1, size, one, 0)
 
     def arrived(recv, sem):
         pltpu.make_async_copy(recv, recv, sem).wait()
@@ -170,12 +159,12 @@
         pltpu.make_async_copy(some, some, sem).wait()
 
     def spread_z(send, recv, send_sem, recv_sem):
-        spread(nz, my_z, on_line, send, recv, send_sem, recv_sem)
+        spread(line, on_line, send, recv, send_sem, recv_sem)
 
     def spread_x(send, recv, send_sem, recv_sem):
-        spread(np_, my_p, in_plane, send, recv, send_sem, recv_sem)
-
-    ZMETA, XMETA, SRC1, SRC2, SRC3, XMIS, ZMIS, FLAG = range(8)
+        spread(plane_ids, in_plane, send, recv, send_sem, recv_sem)
+
+    ZMETA, XMETA, SRC1, SRC2, SRC3, SRC4, MIS, FLAG = range(8)
 
     diagonal = iota((pairs, pairs), 0) == iota((pairs, pairs), 1)
     earlier = iota((pairs, pairs), 0) < iota((pairs, pairs), 1)
@@ -224,47 +213,42 @@
     zmeta = dot(fold_z, coded.astype(BF16)) + jnp.where(iota((nz, 128), 1) == 100, over, 0.0)
     zmeta_send[...] = zmeta.reshape(nz, 1, 128)
 
-    pl.semaphore_wait(barrier, nz - 1 + np_ - 1 + m - 1)
-
-    spread_z(lambda z: zmeta_send.at[z], zmeta_recv, small_s.at[ZMETA], small_r.at[ZMETA])
-    send_z(0)
-    first = min(4, chunks)
-    for q in range(1, first):
-        pack(q)
-        send_z(q)
-    for q in range(first, chunks):
-        pack(q)
-
     unit = math.pi / time_len
     steps = time_len // STEP
     phase_b = ((K0 + iota((STEP, bins), 1)) * iota((STEP, bins), 0)) & (2 * time_len - 1)
     angle_b = phase_b.astype(F32) * unit
     cos_b[...] = jnp.cos(angle_b)
-    sin_b[...] = jnp.sin(angle_b)
+    sin_b[...] = -jnp.sin(angle_b)
     phase_a = ((K0 + iota((steps, bins), 1)) * (iota((steps, bins), 0) * STEP)) & (2 * time_len - 1)
     angle_a = phase_a.astype(F32) * unit
     cos_a[...] = jnp.cos(angle_a).reshape(steps, 1, bins)
-    sin_a[...] = jnp.sin(angle_a).reshape(steps, 1, bins)
-
-    def fill(i, carry):
-        at = pl.ds(pl.multiple_of(i * STEP, STEP), STEP)
-        for q in range(chunks):
-            part = slice(q * PART, (q + 1) * PART)
-            ca, sa = cos_a[i, :, part], sin_a[i, :, part]
-            cb, sb = cos_b[:, part], sin_b[:, part]
-            table[at, 2 * q * PART : (2 * q + 1) * PART] = (ca * cb - sa * sb).astype(BF16)
-            table[at, (2 * q + 1) * PART : (2 * q + 2) * PART] = (-(sa * cb) - ca * sb).astype(BF16)
-        return carry
-
-    lax.fori_loop(0, steps, fill, 0)
-
-    def transform(i, power):
-        at = pl.ds(pl.multiple_of(i * 2 * PART, 2 * PART), 2 * PART)
-        values = dot(rec_ref[...], table[:, at])
-        spec[:, at] = values
-        return power + jnp.sum(values * values, axis=1, keepdims=True)
-
-    power = lax.fori_loop(0, chunks, transform, jnp.zeros((chans, 1), F32))
+    sin_a[...] = -jnp.sin(angle_a).reshape(steps, 1, bins)
+
+    span = 512
+    power = jnp.zeros((chans, 1), F32)
+    for q in range(chunks + 1):
+
+        def step(i, total, q=q):
+            at = pl.ds(pl.multiple_of(i * span, span), span)
+            if q > 0:
+                total = total + dot(rec_ref[:, at], tables[q - 1][at, :])
+            if q < chunks:
+                part = slice(q * PART, (q + 1) * PART)
+                cb, sb = cos_b[:, part], sin_b[:, part]
+                for b in range(span // STEP):
+                    rows = pl.ds(pl.multiple_of(i * span + b * STEP, STEP), STEP)
+                    ca = cos_a[i * (span // STEP) + b, :, part]
+                    sa = sin_a[i * (span // STEP) + b, :, part]
+                    tables[q][rows, 0:PART] = (ca * cb - sa * sb).astype(BF16)
+                    tables[q][rows, PART : 2 * PART] = (sa * cb + ca * sb).astype(BF16)
+            return total
+
+        values = lax.fori_loop(
+            0, time_len // span, step, jnp.zeros((chans, 2 * PART), F32)
+        )
+        if q > 0:
+            spec[:, 2 * (q - 1) * PART : 2 * q * PART] = values
+            power = power + jnp.sum(values * values, axis=1, keepdims=True)
     norm = jnp.sqrt(power / bins + 1e-6)
 
     wanted = jnp.sum(
@@ -277,7 +261,55 @@
         pair = halves(spec[:, 2 * q * PART : (2 * q + 2) * PART] / norm)
         white_hi[q], white_lo[q] = pair
         src_send[q] = dot2(chosen, pair)
+
+    pl.semaphore_wait(barrier, nz - 1 + np_ - 1 + m - 1)
+
     spread_x(lambda p: src_send.at[p], src_mid, small_s.at[SRC1], small_r.at[SRC1])
+    spread_z(lambda z: zmeta_send.at[z], zmeta_recv, small_s.at[ZMETA], small_r.at[ZMETA])
+    send_z(0)
+    for q in range(1, chunks):
+        pack(q)
+
+    def forward_x(q):
+        arrived(z_recv.at[q], zr_sem.at[q])
+        block = jnp.concatenate(
+            [
+                z_recv[q, :, 0:room, :].reshape(z_rows, PART),
+                z_recv[q, :, room : 2 * room, :].reshape(z_rows, PART),
+            ],
+            axis=1,
+        )
+        values = dot2(perm_ref[...], halves(block))
+        x_send[q, :, 0:plane_slots, :] = values[:, :PART].reshape(np_, plane_slots, PART)
+        x_send[q, :, plane_slots : 2 * plane_slots, :] = values[:, PART:].reshape(
+            np_, plane_slots, PART
+        )
+        spread_x(lambda p: x_send.at[q, p], x_recv.at[q], xs_sem.at[q], xr_sem.at[q])
+
+    def name_slots():
+        arrived(xmeta_recv, small_r.at[XMETA])
+        unfold_x = one_hot(lax.div(iota((slots, np_), 0), plane_slots) == iota((slots, np_), 1))
+        metas = xmeta_recv[...].reshape(np_, 128)
+        flag_send[...] = jnp.broadcast_to(
+            jnp.max(jnp.where(iota((np_, 128), 1) == 100, metas, 0.0), keepdims=True), (1, 128)
+        )
+        spread(owners, in_column, lambda y: flag_send, flag_recv, small_s.at[FLAG], small_r.at[FLAG])
+        wide = dot(unfold_x, metas.astype(BF16))
+        lane_x = lax.rem(iota((slots, 128), 0), plane_slots)
+        receiver = lanes_of(wide, lane_x).astype(jnp.int32) - 1
+        source = lanes_of(wide, lane_x + plane_slots).astype(jnp.int32)
+        hits = ones_where(iota((slots, chans), 1) == receiver)
+        g_ref[...] = hits.astype(BF16)
+        gt_ref[...] = hits.T.astype(BF16)
+        h_ref[...] = one_hot((iota((slots, sources), 1) == source) & (receiver >= 0))
+
+    arrived(src_mid, small_r.at[SRC1])
+    part = jnp.sum(src_mid[...], axis=0)
+    few = sources // nz
+    for z in range(nz):
+        src_part[z] = part[z * few : (z + 1) * few]
+    spread_z(lambda z: src_part.at[z], src_line, small_s.at[SRC2], small_r.at[SRC2])
+    send_z(1)
 
     arrived(zmeta_recv, small_r.at[ZMETA])
     unfold_z = one_hot(lax.div(iota((z_rows, nz), 0), room) == iota((z_rows, nz), 1))
@@ -300,55 +332,20 @@
     xmeta_send[...] = xmeta.reshape(np_, 1, 128)
     spread_x(lambda p: xmeta_send.at[p], xmeta_recv, small_s.at[XMETA], small_r.at[XMETA])
 
-    def forward_x(q):
-        arrived(z_recv.at[q], zr_sem.at[q])
-        block = jnp.concatenate(
-            [
-                z_recv[q, :, 0:room, :].reshape(z_rows, PART),
-                z_recv[q, :, room : 2 * room, :].reshape(z_rows, PART),
-            ],
-            axis=1,
-        )
-        values = dot2(perm_ref[...], halves(block))
-        x_send[q, :, 0:plane_slots, :] = values[:, :PART].reshape(np_, plane_slots, PART)
-        x_send[q, :, plane_slots : 2 * plane_slots, :] = values[:, PART:].reshape(
-            np_, plane_slots, PART
-        )
-        spread_x(lambda p: x_send.at[q, p], x_recv.at[q], xs_sem.at[q], xr_sem.at[q])
-
+    arrived(src_line, small_r.at[SRC2])
+    src_own[...] = jnp.sum(src_line[...], axis=0)
+    spread_z(lambda z: src_own, src_rows, small_s.at[SRC3], small_r.at[SRC3])
+    send_z(2)
     forward_x(0)
-
-    arrived(src_mid, small_r.at[SRC1])
-    src_part[...] = jnp.sum(src_mid[...], axis=0)
-    spread_z(lambda z: src_part, src_line, small_s.at[SRC2], small_r.at[SRC2])
-    second = min(6, chunks)
-    for q in range(first, second):
-        send_z(q)
-    for q in range(1, first):
-        forward_x(q)
-
-    arrived(xmeta_recv, small_r.at[XMETA])
-    unfold_x = one_hot(lax.div(iota((slots, np_), 0), plane_slots) == iota((slots, np_), 1))
-    metas = xmeta_recv[...].reshape(np_, 128)
-    flag_send[...] = jnp.broadcast_to(
-        jnp.max(jnp.where(iota((np_, 128), 1) == 100, metas, 0.0), keepdims=True), (1, 128)
-    )
-    spread(m, owner, in_column, lambda y: flag_send, flag_recv, small_s.at[FLAG], small_r.at[FLAG])
-    wide = dot(unfold_x, metas.astype(BF16))
-    lane_x = lax.rem(iota((slots, 128), 0), plane_slots)
-    receiver = lanes_of(wide, lane_x).astype(jnp.int32) - 1
-    source = lanes_of(wide, lane_x + plane_slots).astype(jnp.int32)
-    hits = ones_where(iota((slots, chans), 1) == receiver)
-    g_ref[...] = hits.astype(BF16)
-    gt_ref[...] = hits.T.astype(BF16)
-    h_ref[...] = one_hot((iota((slots, sources), 1) == source) & (receiver >= 0))
-
-    arrived(src_line, small_r.at[SRC2])
-    src_all[...] = jnp.sum(src_line[...], axis=0)
-    spread_x(lambda p: src_all, src_recv, small_s.at[SRC3], small_r.at[SRC3])
-    for q in range(second, chunks):
-        send_z(q)
-    arrived(src_recv, small_r.at[SRC3])
+    name_slots()
+    arrived(src_rows, small_r.at[SRC3])
+    src_all[...] = jnp.concatenate([src_rows[z] for z in range(nz)], axis=0)
+    spread_x(lambda p: src_all, src_recv, small_s.at[SRC4], small_r.at[SRC4])
+    send_z(3)
+    forward_x(1)
+    if chunks > 4:
+        send_z(4)
+    arrived(src_recv, small_r.at[SRC4])
 
     mis_acc[...] = jnp.zeros_like(mis_acc)
 
@@ -369,8 +366,7 @@
         terms = jnp.concatenate([e_re * s_re - e_im * s_im, e_re * s_im + e_im * s_re], axis=1)
         adj_send[q] = dot2(gt_ref[...], halves(terms)).reshape(m, rows_out, 2 * PART)
         spread(
-            m,
-            owner,
+            owners,
             in_column,
             lambda y: adj_send.at[q, y],
             adj_recv.at[q],
@@ -389,7 +385,7 @@
 
         def one(i, carry):
             at = pl.ds(pl.multiple_of(i * span, span), span)
-            product = dot_t(both, table[at, 2 * q * PART : (2 * q + 2) * PART])
+            product = dot_t(both, tables[q][at, :])
             values = product[:rows_out] + product[rows_out:]
             if q == 0:
                 out_ref[:, at] = values
@@ -401,31 +397,36 @@
 
     for q in range(chunks):
         correlate(q)
-        if q + first < chunks:
-            forward_x(q + first)
-        if q >= 2 and q < chunks - 1:
+        if q + 5 < chunks:
+            send_z(q + 5)
+        if q + 2 < chunks:
+            forward_x(q + 2)
+        if 2 <= q < chunks - 1:
             inverse(q - 2)
 
+    lane_4 = iota((slots, 128), 0) & 3
     total = jnp.sum(mis_acc[...], axis=1, keepdims=True) * (0.5 / bins)
-    fold_x = one_hot(iota((np_, slots), 0) == lax.div(iota((np_, slots), 1), plane_slots))
-    spread_out = jnp.where(iota((slots, 128), 1) == lane_x, total, 0.0)
-    xmis_send[...] = dot2(fold_x, halves(spread_out)).reshape(np_, 1, 128)
-    spread_x(lambda p: xmis_send.at[p], xmis_recv, small_s.at[XMIS], small_r.at[XMIS])
-
-    for q in range(max(0, chunks - 3), chunks - 1):
+    count = nz * np_
+    fold_4 = one_hot(iota((count, slots), 0) == (iota((count, slots), 1) >> 2))
+    spread_out = jnp.where(iota((slots, 128), 1) == lane_4, total, 0.0)
+    mis_send[...] = dot2(fold_4, halves(spread_out)).reshape(count, 1, 128)
+
+    spread(
+        [plane_ids[i] * nz + line[j] for i in range(np_) for j in range(nz)],
+        [there(i, j) for i in range(np_) for j in range(nz)],
+        lambda u: mis_send.at[u],
+        mis_recv,
+        small_s.at[MIS],
+        small_r.at[MIS],
+    )
+    for q in range(max(0, chunks - 3), chunks):
         inverse(q)
 
-    arrived(xmis_recv, small_r.at[XMIS])
-    back = dot2(to_plane_hot[:, :np_].astype(BF16), halves(xmis_recv[...].reshape(np_, 128)))
-    spread_out = jnp.where(lane_z == rank_z, lanes_of(back, within), 0.0)
-    zmis_send[...] = dot2(fold_z, halves(spread_out)).reshape(nz, 1, 128)
-    spread_z(lambda z: zmis_send.at[z], zmis_recv, small_s.at[ZMIS], small_r.at[ZMIS])
-
-    inverse(chunks - 1)
-
-    arrived(zmis_recv, small_r.at[ZMIS])
-    back = dot2(unfold_z, halves(zmis_recv[...].reshape(nz, 128)))
-    mis_ref[...] = jnp.sum(pick * lanes_of(back, rank_z), axis=0, keepdims=True)
+    arrived(mis_recv, small_r.at[MIS])
+    unfold_4 = one_hot((iota((slots, count), 0) >> 2) == iota((slots, count), 1))
+    back = dot2(unfold_4, halves(mis_recv[...].reshape(count, 128)))
+    own = ones_where((plane * nz + slab) * CAP + rank == iota((slots, pairs), 0))
+    mis_ref[...] = jnp.sum(own * lanes_of(back, lane_4), axis=0, keepdims=True)
     arrived(flag_recv, small_r.at[FLAG])
     over_ref[...] = jnp.max(flag_recv[...], axis=0)
 
@@ -438,9 +439,9 @@
         (xmeta_recv, XMETA),
         (src_mid, SRC1),
         (src_line, SRC2),
-        (src_recv, SRC3),
-        (xmis_recv, XMIS),
-        (zmis_recv, ZMIS),
+        (src_rows, SRC3),
+        (src_recv, SRC4),
+        (mis_recv, MIS),
         (flag_recv, FLAG),
     ):
         left(recv, small_s.at[sem])
@@ -477,19 +478,19 @@
             vmem((np_, 1, 128), F32),
             vmem((np_, sources, 2 * PART), F32),
             vmem((np_, sources, 2 * PART), F32),
-            vmem((sources, 2 * PART), F32),
-            vmem((nz, sources, 2 * PART), F32),
+            vmem((nz, sources // nz, 2 * PART), F32),
+            vmem((nz, sources // nz, 2 * PART), F32),
+            vmem((sources // nz, 2 * PART), F32),
+            vmem((nz, sources // nz, 2 * PART), F32),
             vmem((sources, 2 * PART), F32),
             vmem((np_, sources, 2 * PART), F32),
             vmem((chunks, m, rows_out, 2 * PART), F32),
             vmem((chunks, m, rows_out, 2 * PART), F32),
-            vmem((np_, 1, 128), F32),
-            vmem((np_, 1, 128), F32),
-            vmem((nz, 1, 128), F32),
-            vmem((nz, 1, 128), F32),
+            vmem((nz * np_, 1, 128), F32),
+            vmem((nz * np_, 1, 128), F32),
             vmem((1, 128), F32),
             vmem((m, 1, 128), F32),
-            vmem((time_len, width), BF16),
+            [vmem((time_len, 2 * PART), BF16) for _ in range(chunks)],
             vmem((time_len // STEP, 1, bins), F32),
             vmem((time_len // STEP, 1, bins), F32),
             vmem((STEP, bins), F32),

time: 76.3 us -> 88.5 us (1.16)
  Pallas kernels: 72.5 us -> 84.8 us
    pallas_call x1, Pallas kernels: 72.5 us -> 84.8 us  [exchange(): pl.pallas_call(functools.partial(kernel, nz, np_, m, room), out_shape=(ja...]
where the time goes in v3:
time: 88.5 us; the launch traced here: 88.4 us
  Pallas kernels  84.8 us (96%)
  local copies, waits for them, and re-layouts  2.64 us (3%)
    pallas_call x1, Pallas kernels, exchange(): pl.pallas_call(functools.partial(kernel, nz, np_, m, room), out_shape=(ja...  84.8 us
    unnamed x16, local copies, waits for them, and re-layouts  2.64 us

profile of v3, /device:TPU:1, one launch (start us, length us, event | category | flops | bytes accessed | tf_op | source)
XLA Modules:
  0.0 88.4 jit_solution(6059240475800815943)
XLA Ops:
  0.6 0.0 copy-start.5
  0.6 0.0 copy-start.2
  0.7 0.0 copy-start.3
  0.7 0.0 copy-start.4
  0.7 0.6 copy-done.5
  1.3 0.0 copy-done.2
  1.3 0.0 copy-done.3
  1.3 0.0 copy-done.4
  1.3 0.0 copy-start
  1.3 0.0 copy-start.1
  1.3 84.8 %shard_map.77 = (f32[32,4096]{1,0:T(8,128)S(1)}, f32[1,128]{1,0:T(1,128)S(1)}, f32[1,128]{1,0:T(1,128)}) custom-call(bf16[128,4096]{1,0:T(8,128)(2,1)} %rec_ref.1, s32[1,16]{1,0:T(1,128)S(1)} %bitcast.7, s32[1,128]{1,0:T(1,128)S(1)} %bitcast.9, s32[1,128]{1,0:T(1,128)S(1)} %bitcast.11, s32[1,128]{1,0:T(1,128)S(1)} %bitcast.13, f32[128,2048]{1,0:T(8,128)} %obs_ref.1), custom_call_target="tpu_custom_call" | custom-call | tf_op jit(solution)/shard_map/pallas_call | solution.py:461
  86.1 0.0 copy-start.6
  86.1 0.7 copy-done.6
  86.8 0.0 copy-done
  86.9 0.0 copy-done.1
  86.9 0.2 conditional.1
  87.1 0.8 copy.14
  87.9 0.5 copy.15
Async XLA Ops:
  0.6 0.7 copy-start.5
  0.6 0.7 copy-start.2
  0.7 0.7 copy-start.3
  0.7 0.7 copy-start.4
  1.3 85.5 %copy-start = (bf16[128,4096]{1,0:T(8,128)(2,1)S(1)}, bf16[128,4096]{1,0:T(8,128)(2,1)}, u32[]{:S(2)}) copy-start(bf16[128,4096]{1,0:T(8,128)(2,1)} %rec_ref.1) | copy-start | bytes 3145732
  1.3 85.5 %copy-start.1 = (f32[128,2048]{1,0:T(8,128)S(1)}, f32[128,2048]{1,0:T(8,128)}, u32[]{:S(2)}) copy-start(f32[128,2048]{1,0:T(8,128)} %obs_ref.1) | copy-start | bytes 3145732
  86.1 0.7 copy-start.6

commit v4 on v3

--- a/solution.py
+++ b/solution.py
@@ -86,14 +86,14 @@
     mis_recv,
     flag_send,
     flag_recv,
+    rec_halves,
     tables,
     cos_a,
     sin_a,
     cos_b,
     sin_b,
     spec,
-    white_hi,
-    white_lo,
+    white,
     perm_ref,
     g_ref,
     gt_ref,
@@ -178,7 +178,7 @@
     over = jnp.max(jnp.where(place >= room, 1.0, 0.0), axis=1, keepdims=True)
     row = jnp.where(place < room, slab * room + place, -1)
     pick = ones_where(row == iota((z_rows, pairs), 0))
-    pick_bf = pick.astype(BF16)
+    pick_bf = jnp.concatenate([pick, pick], axis=1).astype(BF16)
 
     def pack(q):
         block = jnp.concatenate(
@@ -188,7 +188,7 @@
             ],
             axis=1,
         )
-        values = dot2(pick_bf, halves(block))
+        values = dot(pick_bf, jnp.concatenate(halves(block), axis=0))
         z_send[q, :, 0:room, :] = values[:, :PART].reshape(nz, room, PART)
         z_send[q, :, room : 2 * room, :] = values[:, PART:].reshape(nz, room, PART)
 
@@ -213,42 +213,58 @@
     zmeta = dot(fold_z, coded.astype(BF16)) + jnp.where(iota((nz, 128), 1) == 100, over, 0.0)
     zmeta_send[...] = zmeta.reshape(nz, 1, 128)
 
-    unit = math.pi / time_len
-    steps = time_len // STEP
-    phase_b = ((K0 + iota((STEP, bins), 1)) * iota((STEP, bins), 0)) & (2 * time_len - 1)
-    angle_b = phase_b.astype(F32) * unit
-    cos_b[...] = jnp.cos(angle_b)
-    sin_b[...] = -jnp.sin(angle_b)
-    phase_a = ((K0 + iota((steps, bins), 1)) * (iota((steps, bins), 0) * STEP)) & (2 * time_len - 1)
-    angle_a = phase_a.astype(F32) * unit
-    cos_a[...] = jnp.cos(angle_a).reshape(steps, 1, bins)
-    sin_a[...] = -jnp.sin(angle_a).reshape(steps, 1, bins)
-
-    span = 512
+    half = time_len // 2
+    steps = half // STEP
+    digit = iota((32, bins), 0) >> 3
+    times = (iota((32, bins), 0) & 7) * jnp.where(
+        digit == 0, 1, jnp.where(digit == 1, 8, jnp.where(digit == 2, 64, 512))
+    )
+    phase = ((K0 + iota((32, bins), 1)) * times) & (2 * time_len - 1)
+    angle = phase.astype(F32) * (math.pi / time_len)
+    cos_d, sin_d = jnp.cos(angle), -jnp.sin(angle)
+    for j in range(8):
+        cj, sj = cos_d[8 + j : 9 + j], sin_d[8 + j : 9 + j]
+        cos_b[8 * j : 8 * j + 8, :] = cj * cos_d[:8] - sj * sin_d[:8]
+        sin_b[8 * j : 8 * j + 8, :] = sj * cos_d[:8] + cj * sin_d[:8]
+    for j in range(steps // 8):
+        cj, sj = cos_d[24 + j : 25 + j], sin_d[24 + j : 25 + j]
+        cos_a[8 * j : 8 * j + 8] = (cj * cos_d[16:24] - sj * sin_d[16:24]).reshape(8, 1, bins)
+        sin_a[8 * j : 8 * j + 8] = (sj * cos_d[16:24] + cj * sin_d[16:24]).reshape(8, 1, bins)
+
+    turn = iota((1, PART), 1) & 3
+    keep = jnp.where(turn == 0, 1.0, jnp.where(turn == 2, -1.0, 0.0))
+    swap = jnp.where(turn == 1, 1.0, jnp.where(turn == 3, -1.0, 0.0))
+    rec_halves[0:chans, :] = rec_ref[:, 0:half]
+    rec_halves[chans : 2 * chans, :] = rec_ref[:, half:time_len]
+
+    def fill(i, carry):
+        at = pl.ds(pl.multiple_of(i * STEP, STEP), STEP)
+        for q in range(chunks):
+            part = slice(q * PART, (q + 1) * PART)
+            ca, sa = cos_a[i, :, part], sin_a[i, :, part]
+            cb, sb = cos_b[:, part], sin_b[:, part]
+            tables[q][at, 0:PART] = (ca * cb - sa * sb).astype(BF16)
+            tables[q][at, PART : 2 * PART] = (sa * cb + ca * sb).astype(BF16)
+        return carry
+
+    lax.fori_loop(0, steps, fill, 0)
+
+    pl.semaphore_wait(barrier, nz - 1 + np_ - 1 + m - 1)
+
+    spread_z(lambda z: zmeta_send.at[z], zmeta_recv, small_s.at[ZMETA], small_r.at[ZMETA])
+    send_z(0)
+    pack(1)
+    send_z(1)
+
     power = jnp.zeros((chans, 1), F32)
-    for q in range(chunks + 1):
-
-        def step(i, total, q=q):
-            at = pl.ds(pl.multiple_of(i * span, span), span)
-            if q > 0:
-                total = total + dot(rec_ref[:, at], tables[q - 1][at, :])
-            if q < chunks:
-                part = slice(q * PART, (q + 1) * PART)
-                cb, sb = cos_b[:, part], sin_b[:, part]
-                for b in range(span // STEP):
-                    rows = pl.ds(pl.multiple_of(i * span + b * STEP, STEP), STEP)
-                    ca = cos_a[i * (span // STEP) + b, :, part]
-                    sa = sin_a[i * (span // STEP) + b, :, part]
-                    tables[q][rows, 0:PART] = (ca * cb - sa * sb).astype(BF16)
-                    tables[q][rows, PART : 2 * PART] = (sa * cb + ca * sb).astype(BF16)
-            return total
-
-        values = lax.fori_loop(
-            0, time_len // span, step, jnp.zeros((chans, 2 * PART), F32)
-        )
-        if q > 0:
-            spec[:, 2 * (q - 1) * PART : 2 * q * PART] = values
-            power = power + jnp.sum(values * values, axis=1, keepdims=True)
+    for q in range(chunks):
+        sums = dot(rec_halves[...], tables[q][...])
+        late_re, late_im = sums[chans:, :PART], sums[chans:, PART:]
+        values = sums[:chans] + jnp.concatenate(
+            [keep * late_re + swap * late_im, keep * late_im - swap * late_re], axis=1
+        )
+        spec[:, 2 * q * PART : 2 * (q + 1) * PART] = values
+        power = power + jnp.sum(values * values, axis=1, keepdims=True)
     norm = jnp.sqrt(power / bins + 1e-6)
 
     wanted = jnp.sum(
@@ -259,15 +275,11 @@
     chosen = one_hot(iota((sources, chans), 1) == wanted - me * chans)
     for q in range(chunks):
         pair = halves(spec[:, 2 * q * PART : (2 * q + 2) * PART] / norm)
-        white_hi[q], white_lo[q] = pair
+        white[q, 0:chans, :], white[q, chans : 2 * chans, :] = pair
         src_send[q] = dot2(chosen, pair)
 
-    pl.semaphore_wait(barrier, nz - 1 + np_ - 1 + m - 1)
-
     spread_x(lambda p: src_send.at[p], src_mid, small_s.at[SRC1], small_r.at[SRC1])
-    spread_z(lambda z: zmeta_send.at[z], zmeta_recv, small_s.at[ZMETA], small_r.at[ZMETA])
-    send_z(0)
-    for q in range(1, chunks):
+    for q in range(2, chunks):
         pack(q)
 
     def forward_x(q):
@@ -299,9 +311,11 @@
         receiver = lanes_of(wide, lane_x).astype(jnp.int32) - 1
         source = lanes_of(wide, lane_x + plane_slots).astype(jnp.int32)
         hits = ones_where(iota((slots, chans), 1) == receiver)
-        g_ref[...] = hits.astype(BF16)
+        g_ref[:, 0:chans] = hits.astype(BF16)
+        g_ref[:, chans : 2 * chans] = hits.astype(BF16)
         gt_ref[...] = hits.T.astype(BF16)
-        h_ref[...] = one_hot((iota((slots, sources), 1) == source) & (receiver >= 0))
+        named = lax.rem(iota((slots, 2 * sources), 1), sources) == source
+        h_ref[...] = one_hot(named & (receiver >= 0))
 
     arrived(src_mid, small_r.at[SRC1])
     part = jnp.sum(src_mid[...], axis=0)
@@ -309,7 +323,7 @@
     for z in range(nz):
         src_part[z] = part[z * few : (z + 1) * few]
     spread_z(lambda z: src_part.at[z], src_line, small_s.at[SRC2], small_r.at[SRC2])
-    send_z(1)
+    send_z(2)
 
     arrived(zmeta_recv, small_r.at[ZMETA])
     unfold_z = one_hot(lax.div(iota((z_rows, nz), 0), room) == iota((z_rows, nz), 1))
@@ -335,16 +349,15 @@
     arrived(src_line, small_r.at[SRC2])
     src_own[...] = jnp.sum(src_line[...], axis=0)
     spread_z(lambda z: src_own, src_rows, small_s.at[SRC3], small_r.at[SRC3])
-    send_z(2)
+    send_z(3)
     forward_x(0)
     name_slots()
     arrived(src_rows, small_r.at[SRC3])
     src_all[...] = jnp.concatenate([src_rows[z] for z in range(nz)], axis=0)
     spread_x(lambda p: src_all, src_recv, small_s.at[SRC4], small_r.at[SRC4])
-    send_z(3)
+    for q in range(4, min(6, chunks)):
+        send_z(q)
     forward_x(1)
-    if chunks > 4:
-        send_z(4)
     arrived(src_recv, small_r.at[SRC4])
 
     mis_acc[...] = jnp.zeros_like(mis_acc)
@@ -353,8 +366,8 @@
         arrived(x_recv.at[q], xr_sem.at[q])
         band = (q * PART + iota((1, PART), 1)).astype(F32)
         taper = 0.5 - 0.5 * jnp.cos((band + 0.5) * (2.0 * math.pi / bins))
-        source_rows = dot2(h_ref[...], halves(src_recv[q]))
-        receiver_rows = dot2(g_ref[...], (white_hi[q], white_lo[q]))
+        source_rows = dot(h_ref[...], jnp.concatenate(halves(src_recv[q]), axis=0))
+        receiver_rows = dot(g_ref[...], white[q])
         s_re, s_im = source_rows[:, :PART], source_rows[:, PART:]
         r_re, r_im = receiver_rows[:, :PART], receiver_rows[:, PART:]
         d_re = s_re * r_re + s_im * r_im - x_recv[q, :, 0:plane_slots, :].reshape(slots, PART)
@@ -379,26 +392,33 @@
         total = adj_recv[q, 0]
         for y in range(1, m):
             total = total + adj_recv[q, y]
-        high, low = halves(total * (1.0 / math.sqrt(bins)))
-        both = jnp.concatenate([high, low], axis=0)
-        span = min(512, time_len)
+        total = total * (1.0 / math.sqrt(bins))
+        real, imaginary = total[:, :PART], total[:, PART:]
+        late = jnp.concatenate(
+            [keep * real - swap * imaginary, swap * real + keep * imaginary], axis=1
+        )
+        both = jnp.concatenate(halves(jnp.concatenate([total, late], axis=0)), axis=0)
+        span = min(512, half)
 
         def one(i, carry):
             at = pl.ds(pl.multiple_of(i * span, span), span)
+            after = pl.ds(pl.multiple_of(half + i * span, span), span)
             product = dot_t(both, tables[q][at, :])
-            values = product[:rows_out] + product[rows_out:]
+            values = product[: 2 * rows_out] + product[2 * rows_out :]
             if q == 0:
-                out_ref[:, at] = values
+                out_ref[:, at] = values[:rows_out]
+                out_ref[:, after] = values[rows_out:]
             else:
-                out_ref[:, at] += values
+                out_ref[:, at] += values[:rows_out]
+                out_ref[:, after] += values[rows_out:]
             return carry
 
-        lax.fori_loop(0, time_len // span, one, 0)
+        lax.fori_loop(0, half // span, one, 0)
 
     for q in range(chunks):
         correlate(q)
-        if q + 5 < chunks:
-            send_z(q + 5)
+        if q + 6 < chunks:
+            send_z(q + 6)
         if q + 2 < chunks:
             forward_x(q + 2)
         if 2 <= q < chunks - 1:
@@ -490,18 +510,18 @@
             vmem((nz * np_, 1, 128), F32),
             vmem((1, 128), F32),
             vmem((m, 1, 128), F32),
-            [vmem((time_len, 2 * PART), BF16) for _ in range(chunks)],
-            vmem((time_len // STEP, 1, bins), F32),
-            vmem((time_len // STEP, 1, bins), F32),
+            vmem((2 * chans, time_len // 2), BF16),
+            [vmem((time_len // 2, 2 * PART), BF16) for _ in range(chunks)],
+            vmem((time_len // 2 // STEP, 1, bins), F32),
+            vmem((time_len // 2 // STEP, 1, bins), F32),
             vmem((STEP, bins), F32),
             vmem((STEP, bins), F32),
             vmem((chans, width), F32),
-            vmem((chunks, chans, 2 * PART), BF16),
-            vmem((chunks, chans, 2 * PART), BF16),
+            vmem((chunks, 2 * chans, 2 * PART), BF16),
             vmem((slots, nz * room), BF16),
-            vmem((slots, chans), BF16),
+            vmem((slots, 2 * chans), BF16),
             vmem((chans, slots), BF16),
-            vmem((slots, sources), BF16),
+            vmem((slots, 2 * sources), BF16),
             vmem((slots, PART), F32),
             pltpu.SemaphoreType.DMA((chunks,)),
             pltpu.SemaphoreType.DMA((chunks,)),

time: 88.5 us -> 66.8 us (0.75)
  Pallas kernels: 84.8 us -> 63.2 us
    pallas_call x1, Pallas kernels: 84.8 us -> 63.2 us  [exchange(): pl.pallas_call(functools.partial(kernel, nz, np_, m, room), out_shape=(ja...]
where the time goes in v4:
time: 66.8 us; the launch traced here: 66.7 us
  Pallas kernels  63.2 us (95%)
  local copies, waits for them, and re-layouts  2.64 us (4%)
  between operations  0.75 us (1%)
    pallas_call x1, Pallas kernels, exchange(): pl.pallas_call(functools.partial(kernel, nz, np_, m, room), out_shape=(ja...  63.2 us
    unnamed x16, local copies, waits for them, and re-layouts  2.64 us

profile of v4, /device:TPU:1, one launch (start us, length us, event | category | flops | bytes accessed | tf_op | source)
XLA Modules:
  0.0 66.7 jit_solution(12225568330831432559)
XLA Ops:
  0.6 0.0 copy-start.5
  0.6 0.0 copy-start.2
  0.7 0.0 copy-start.3
  0.7 0.0 copy-start.4
  0.7 0.6 copy-done.5
  1.3 0.0 copy-done.2
  1.3 0.0 copy-done.3
  1.3 0.0 copy-done.4
  1.3 0.0 copy-start
  1.3 0.0 copy-start.1
  1.3 63.2 %shard_map.77 = (f32[32,4096]{1,0:T(8,128)S(1)}, f32[1,128]{1,0:T(1,128)S(1)}, f32[1,128]{1,0:T(1,128)}) custom-call(bf16[128,4096]{1,0:T(8,128)(2,1)} %rec_ref.1, s32[1,16]{1,0:T(1,128)S(1)} %bitcast.7, s32[1,128]{1,0:T(1,128)S(1)} %bitcast.9, s32[1,128]{1,0:T(1,128)S(1)} %bitcast.11, s32[1,128]{1,0:T(1,128)S(1)} %bitcast.13, f32[128,2048]{1,0:T(8,128)} %obs_ref.1), custom_call_target="tpu_custom_call" | custom-call | tf_op jit(solution)/shard_map/pallas_call | solution.py:481
  64.5 0.0 copy-start.6
  64.5 0.7 copy-done.6
  65.2 0.0 copy-done
  65.2 0.0 copy-done.1
  65.2 0.2 conditional.1
  65.4 0.8 %copy.14 = f32[32,4096]{1,0:T(8,128)} copy(f32[32,4096]{1,0:T(8,128)S(1)} %get-tuple-element.45) | data formatting | bytes 1048576
  66.2 0.5 copy.15
Async XLA Ops:
  0.6 0.7 copy-start.5
  0.6 0.7 copy-start.2
  0.7 0.7 %copy-start.3 = (s32[128,1]{0,1:T(1,128)S(1)}, s32[128,1]{0,1:T(1,128)}, u32[]{:S(2)}) copy-start(s32[128,1]{0,1:T(1,128)} %param.10) | copy-start | bytes 1540
  0.7 0.7 %copy-start.4 = (s32[128]{0:T(128)S(1)}, s32[128]{0:T(128)}, u32[]{:S(2)}) copy-start(s32[128]{0:T(128)} %param.11) | copy-start | bytes 1540
  1.3 63.9 %copy-start = (bf16[128,4096]{1,0:T(8,128)(2,1)S(1)}, bf16[128,4096]{1,0:T(8,128)(2,1)}, u32[]{:S(2)}) copy-start(bf16[128,4096]{1,0:T(8,128)(2,1)} %rec_ref.1) | copy-start | bytes 3145732
  1.3 63.9 %copy-start.1 = (f32[128,2048]{1,0:T(8,128)S(1)}, f32[128,2048]{1,0:T(8,128)}, u32[]{:S(2)}) copy-start(f32[128,2048]{1,0:T(8,128)} %obs_ref.1) | copy-start | bytes 3145732
  64.5 0.7 copy-start.6

commit v5 on v4

--- a/solution.py
+++ b/solution.py
@@ -44,6 +44,13 @@
 
 def dot2(left, pair):
     return dot(left, pair[0]) + dot(left, pair[1])
+
+
+def both_ways(size):
+    steps = [0]
+    for i in range(1, size // 2 + 1):
+        steps += [i] if 2 * i == size else [i, size - i]
+    return steps
 
 
 def lanes_of(values, lane):
@@ -121,8 +128,14 @@
     owner = lax.axis_index("src")
     my_z = lax.rem(lax.div(me, 2), nz)
     my_p = lax.div(me, 2 * nz) * 2 + lax.rem(me, 2)
-    line = [lax.rem(my_z + i, nz) for i in range(nz)]
-    plane_ids = [lax.rem(my_p + i, np_) for i in range(np_)]
+    nx = np_ // 2
+    my_x, my_core = lax.div(me, 2 * nz), lax.rem(me, 2)
+    line = [lax.rem(my_z + i, nz) for i in both_ways(nz)]
+    plane_ids = [
+        lax.rem(my_x + i, nx) * 2 + lax.rem(my_core + c, 2)
+        for i in both_ways(nx)
+        for c in range(2)
+    ]
     owners = [lax.rem(owner + i, m) for i in range(m)]
     base = [lax.div(p, 2) * (2 * nz) + lax.rem(p, 2) for p in plane_ids]
 
@@ -351,13 +364,14 @@
     spread_z(lambda z: src_own, src_rows, small_s.at[SRC3], small_r.at[SRC3])
     send_z(3)
     forward_x(0)
+    forward_x(1)
     name_slots()
     arrived(src_rows, small_r.at[SRC3])
     src_all[...] = jnp.concatenate([src_rows[z] for z in range(nz)], axis=0)
     spread_x(lambda p: src_all, src_recv, small_s.at[SRC4], small_r.at[SRC4])
     for q in range(4, min(6, chunks)):
         send_z(q)
-    forward_x(1)
+    forward_x(2)
     arrived(src_recv, small_r.at[SRC4])
 
     mis_acc[...] = jnp.zeros_like(mis_acc)
@@ -419,8 +433,8 @@
         correlate(q)
         if q + 6 < chunks:
             send_z(q + 6)
-        if q + 2 < chunks:
-            forward_x(q + 2)
+        if q + 3 < chunks:
+            forward_x(q + 3)
         if 2 <= q < chunks - 1:
             inverse(q - 2)
 

time: 66.8 us -> 66.6 us (level)
  no operation moved by 1% of the time
where the time goes in v5:
time: 66.6 us; the launch traced here: 66.5 us
  Pallas kernels  62.9 us (94%)
  local copies, waits for them, and re-layouts  2.64 us (4%)
  between operations  0.75 us (1%)
    pallas_call x1, Pallas kernels, exchange(): pl.pallas_call(functools.partial(kernel, nz, np_, m, room), out_shape=(ja...  62.9 us
    unnamed x16, local copies, waits for them, and re-layouts  2.64 us

profile of v5, /device:TPU:1, one launch (start us, length us, event | category | flops | bytes accessed | tf_op | source)
XLA Modules:
  0.0 66.5 jit_solution(4269138481452217547)
XLA Ops:
  0.6 0.0 copy-start.5
  0.6 0.0 copy-start.2
  0.7 0.0 copy-start.3
  0.7 0.0 copy-start.4
  0.7 0.6 copy-done.5
  1.3 0.0 copy-done.2
  1.3 0.0 copy-done.3
  1.3 0.0 copy-done.4
  1.3 0.0 copy-start
  1.3 0.0 copy-start.1
  1.3 62.9 %shard_map.77 = (f32[32,4096]{1,0:T(8,128)S(1)}, f32[1,128]{1,0:T(1,128)S(1)}, f32[1,128]{1,0:T(1,128)}) custom-call(bf16[128,4096]{1,0:T(8,128)(2,1)} %rec_ref.1, s32[1,16]{1,0:T(1,128)S(1)} %bitcast.7, s32[1,128]{1,0:T(1,128)S(1)} %bitcast.9, s32[1,128]{1,0:T(1,128)S(1)} %bitcast.11, s32[1,128]{1,0:T(1,128)S(1)} %bitcast.13, f32[128,2048]{1,0:T(8,128)} %obs_ref.1), custom_call_target="tpu_custom_call" | custom-call | tf_op jit(solution)/shard_map/pallas_call | solution.py:495
  64.2 0.0 copy-start.6
  64.3 0.7 copy-done.6
  65.0 0.0 copy-done
  65.0 0.0 copy-done.1
  65.0 0.2 conditional.1
  65.2 0.8 %copy.14 = f32[32,4096]{1,0:T(8,128)} copy(f32[32,4096]{1,0:T(8,128)S(1)} %get-tuple-element.45) | data formatting | bytes 1048576
  66.0 0.5 copy.15
Async XLA Ops:
  0.6 0.7 copy-start.5
  0.6 0.7 copy-start.2
  0.7 0.7 %copy-start.3 = (s32[128,1]{0,1:T(1,128)S(1)}, s32[128,1]{0,1:T(1,128)}, u32[]{:S(2)}) copy-start(s32[128,1]{0,1:T(1,128)} %param.10) | copy-start | bytes 1540
  0.7 0.7 %copy-start.4 = (s32[128]{0:T(128)S(1)}, s32[128]{0:T(128)}, u32[]{:S(2)}) copy-start(s32[128]{0:T(128)} %param.11) | copy-start | bytes 1540
  1.3 63.6 %copy-start = (bf16[128,4096]{1,0:T(8,128)(2,1)S(1)}, bf16[128,4096]{1,0:T(8,128)(2,1)}, u32[]{:S(2)}) copy-start(bf16[128,4096]{1,0:T(8,128)(2,1)} %rec_ref.1) | copy-start | bytes 3145732
  1.3 63.6 %copy-start.1 = (f32[128,2048]{1,0:T(8,128)S(1)}, f32[128,2048]{1,0:T(8,128)}, u32[]{:S(2)}) copy-start(f32[128,2048]{1,0:T(8,128)} %obs_ref.1) | copy-start | bytes 3145732
  64.2 0.7 %copy-start.6 = (f32[1,128]{1,0:T(1,128)S(1)}, f32[1,128]{1,0:T(1,128)}, u32[]{:S(2)}) copy-start(f32[1,128]{1,0:T(1,128)} %get-tuple-element.34) | copy-start | bytes 1540

commit v6 on v5

--- a/solution.py
+++ b/solution.py
@@ -209,6 +209,7 @@
         spread_z(lambda z: z_send.at[q, z], z_recv.at[q], zs_sem.at[q], zr_sem.at[q])
 
     pack(0)
+    pack(1)
     lane_z = iota((z_rows, 128), 1)
     rank_z = lax.rem(iota((z_rows, 128), 0), room)
 
@@ -266,7 +267,6 @@
 
     spread_z(lambda z: zmeta_send.at[z], zmeta_recv, small_s.at[ZMETA], small_r.at[ZMETA])
     send_z(0)
-    pack(1)
     send_z(1)
 
     power = jnp.zeros((chans, 1), F32)
@@ -430,13 +430,13 @@
         lax.fori_loop(0, half // span, one, 0)
 
     for q in range(chunks):
-        correlate(q)
         if q + 6 < chunks:
             send_z(q + 6)
+        correlate(q)
         if q + 3 < chunks:
             forward_x(q + 3)
-        if 2 <= q < chunks - 1:
-            inverse(q - 2)
+        if 3 <= q < chunks - 1:
+            inverse(q - 3)
 
     lane_4 = iota((slots, 128), 0) & 3
     total = jnp.sum(mis_acc[...], axis=1, keepdims=True) * (0.5 / bins)
@@ -453,14 +453,14 @@
         small_s.at[MIS],
         small_r.at[MIS],
     )
-    for q in range(max(0, chunks - 3), chunks):
+    for q in range(max(0, chunks - 4), chunks):
         inverse(q)
 
     arrived(mis_recv, small_r.at[MIS])
     unfold_4 = one_hot((iota((slots, count), 0) >> 2) == iota((slots, count), 1))
     back = dot2(unfold_4, halves(mis_recv[...].reshape(count, 128)))
     own = ones_where((plane * nz + slab) * CAP + rank == iota((slots, pairs), 0))
-    mis_ref[...] = jnp.sum(own * lanes_of(back, lane_4), axis=0, keepdims=True)
+    mis_ref[...] = jnp.sum(own * lanes_of(back, lane_4), axis=0)
     arrived(flag_recv, small_r.at[FLAG])
     over_ref[...] = jnp.max(flag_recv[...], axis=0)
 
@@ -496,7 +496,7 @@
         functools.partial(kernel, nz, np_, m, room),
         out_shape=(
             jax.ShapeDtypeStruct((rows_out, time_len), F32),
-            jax.ShapeDtypeStruct((1, pairs), F32),
+            jax.ShapeDtypeStruct((pairs,), F32),
             jax.ShapeDtypeStruct((1, 128), F32),
         ),
         in_specs=[pl.BlockSpec(memory_space=vmem)] * 6,
@@ -573,7 +573,7 @@
         lambda held: held,
         (adjoint, misfit),
     )
-    return adjoint, misfit.reshape(pairs)
+    return adjoint, misfit
 
 
 def solution(mesh):

time: 66.6 us -> 66.2 us (level)
  no operation moved by 1% of the time
where the time goes in v6:
time: 66.2 us; the launch traced here: 66.1 us
  Pallas kernels  62.6 us (95%)
  local copies, waits for them, and re-layouts  2.64 us (4%)
  between operations  0.75 us (1%)
    pallas_call x1, Pallas kernels, exchange(): pl.pallas_call(functools.partial(kernel, nz, np_, m, room), out_shape=(ja...  62.6 us
    unnamed x16, local copies, waits for them, and re-layouts  2.64 us

profile of v6, /device:TPU:1, one launch (start us, length us, event | category | flops | bytes accessed | tf_op | source)
XLA Modules:
  0.0 66.1 jit_solution(1742554784934663077)
XLA Ops:
  0.6 0.0 copy-start.5
  0.6 0.0 copy-start.2
  0.7 0.0 copy-start.3
  0.7 0.0 copy-start.4
  0.7 0.6 copy-done.5
  1.3 0.0 copy-done.2
  1.3 0.0 copy-done.3
  1.3 0.0 copy-done.4
  1.3 0.0 copy-start
  1.3 0.0 copy-start.1
  1.3 62.6 %shard_map.81 = (f32[32,4096]{1,0:T(8,128)S(1)}, f32[128]{0:T(128)S(1)}, f32[1,128]{1,0:T(1,128)}) custom-call(bf16[128,4096]{1,0:T(8,128)(2,1)} %rec_ref.1, s32[1,16]{1,0:T(1,128)S(1)} %bitcast.6, s32[1,128]{1,0:T(1,128)S(1)} %bitcast.8, s32[1,128]{1,0:T(1,128)S(1)} %bitcast.10, s32[1,128]{1,0:T(1,128)S(1)} %bitcast.12, f32[128,2048]{1,0:T(8,128)} %obs_ref.1), custom_call_target="tpu_custom_call" | custom-call | tf_op jit(solution)/shard_map/pallas_call | solution.py:495
  63.9 0.0 copy-start.6
  63.9 0.7 copy-done.6
  64.6 0.0 copy-done
  64.6 0.0 copy-done.1
  64.6 0.2 conditional.1
  64.8 0.8 %copy.18 = f32[32,4096]{1,0:T(8,128)} copy(f32[32,4096]{1,0:T(8,128)S(1)} %get-tuple-element.42) | data formatting | bytes 1048576
  65.6 0.5 copy.19
Async XLA Ops:
  0.6 0.7 copy-start.5
  0.6 0.7 %copy-start.2 = (s32[16]{0:T(128)S(1)}, s32[16]{0:T(128)}, u32[]{:S(2)}) copy-start(s32[16]{0:T(128)} %param.9) | copy-start | bytes 196
  0.7 0.7 %copy-start.3 = (s32[128,1]{0,1:T(1,128)S(1)}, s32[128,1]{0,1:T(1,128)}, u32[]{:S(2)}) copy-start(s32[128,1]{0,1:T(1,128)} %param.10) | copy-start | bytes 1540
  0.7 0.7 %copy-start.4 = (s32[128]{0:T(128)S(1)}, s32[128]{0:T(128)}, u32[]{:S(2)}) copy-start(s32[128]{0:T(128)} %param.11) | copy-start | bytes 1540
  1.3 63.3 %copy-start = (bf16[128,4096]{1,0:T(8,128)(2,1)S(1)}, bf16[128,4096]{1,0:T(8,128)(2,1)}, u32[]{:S(2)}) copy-start(bf16[128,4096]{1,0:T(8,128)(2,1)} %rec_ref.1) | copy-start | bytes 3145732
  1.3 63.3 %copy-start.1 = (f32[128,2048]{1,0:T(8,128)S(1)}, f32[128,2048]{1,0:T(8,128)}, u32[]{:S(2)}) copy-start(f32[128,2048]{1,0:T(8,128)} %obs_ref.1) | copy-start | bytes 3145732
  63.9 0.7 %copy-start.6 = (f32[1,128]{1,0:T(1,128)S(1)}, f32[1,128]{1,0:T(1,128)}, u32[]{:S(2)}) copy-start(f32[1,128]{1,0:T(1,128)} %get-tuple-element.29) | copy-start | bytes 1540
